TPU v7x, 256 devices: a whole 4x4x8 slice. The times are simulated.
256 devices in a mesh: row: 8 (over x, core), col: 32 (over y, z).
Axes of the slice: x: 4, y: 4, z: 8, core: 2. Of those that a mesh axis runs over, the one named last changes fastest.
Arguments:
- positions: float32 [3, 524288], P(None, ('row', 'col')), may hold values from 0 to 649
- velocities: float32 [3, 524288], P(None, ('row', 'col')), may hold values from -6 to 6
- chain_order: int32 [4096, 128], P(('row', 'col')), may hold values from 0 to 127, as said below
- tile_list: int32 [2, 20480], P(None, ('row', 'col')), may hold values from 0 to 511, as said below
Outputs:
- new_velocity: float32 [3, 524288], P(None, ('row', 'col'))
- new_position: float32 [3, 524288], P(None, ('row', 'col'))
Inputs may be any that keep to these rules, and one draw needn't show every extreme that they name: `chain_order`: each row is a permutation of 0 to 127. `tile_list`: the first row names a block of the row group, below 512; the second a block of the column group, below 128; for k = 0 to 15, tile k of device (p, q) pairs that device's own block k with itself, its entries being q * 16 + k and p * 16 + k.
All inputs are finite; a program needn't handle non-finite values.
Results may differ from a plain program's by a relative error of at most 0.0003.
Values sent between devices are 32-bit elements; how exact they have to be, the bound alone decides.
A program may use at most 128 MiB of HBM per device.

v0:
```python
import jax
import jax.numpy as jnp
from jax import lax
from jax.sharding import PartitionSpec as P

BLK = 128
CHAIN = 32
LINES_X = 4
LINES_Y = 4


cutoff = 2.5
spacing = 1.1
spring = 30.0
bond_reach = 1.5
time_step = 0.005
shift_force = 24.0 * (2.0 * cutoff ** (-13) - cutoff ** (-7))


def pair_terms(row_atoms, column_atoms, same_block, periods):
    offset = row_atoms[:, :, None] - column_atoms[:, None, :]
    offset = offset - periods * jnp.floor(offset / periods + 0.5)
    squared = jnp.sum(offset * offset, axis=0)
    atom_count = row_atoms.shape[1]
    diagonal = jnp.eye(atom_count, dtype=bool) & same_block
    inside = (squared < cutoff * cutoff) & jnp.logical_not(diagonal)
    guarded = jnp.where(diagonal, 1.0, squared)
    inverse = 1.0 / guarded
    cubed = inverse * inverse * inverse
    magnitude = 24.0 * inverse * cubed * (2.0 * cubed - 1.0) - shift_force * jnp.sqrt(inverse)
    magnitude = jnp.where(inside, magnitude, 0.0)
    pair_force = offset * magnitude[None]
    keep_column = jnp.where(same_block, 0.0, 1.0)
    return (jnp.sum(pair_force, axis=2), -jnp.sum(pair_force, axis=1) * keep_column)


def fene(block_positions, chain):
    block_count = block_positions.shape[1]
    ordered = jnp.take_along_axis(block_positions, chain[None], axis=2)
    bond_vector = ordered[:, :, 1:] - ordered[:, :, :-1]
    squared = jnp.sum(bond_vector * bond_vector, axis=0)
    rank_next = jnp.arange(1, BLK, dtype=jnp.int32)
    bonded = rank_next % CHAIN != 0
    coefficient = -spring / jnp.maximum(1.0 - squared / (bond_reach * bond_reach), 0.3)
    coefficient = jnp.where(bonded[None, :], coefficient, 0.0)
    pulled = bond_vector * coefficient[None]
    chain_force = jnp.pad(pulled, ((0, 0), (0, 0), (1, 0))) - jnp.pad(
        pulled, ((0, 0), (0, 0), (0, 1))
    )
    block_rows = jnp.arange(block_count, dtype=jnp.int32)[:, None]
    return jnp.zeros_like(block_positions).at[:, block_rows, chain].set(chain_force)


def on_device(positions, velocities, chain_order, tile_list):
    row_count = lax.axis_size("row")
    column_count = lax.axis_size("col")
    row_index = lax.axis_index("row")
    column_index = lax.axis_index("col")
    owned_blocks = positions.shape[1] // BLK
    periods = jnp.asarray(
        [
            4.0 * spacing * LINES_X * column_count,
            4.0 * spacing * LINES_Y * row_count,
            8.0 * spacing,
        ],
        jnp.float32,
    ).reshape(3, 1, 1)
    paired = jax.vmap(pair_terms, in_axes=(1, 1, 0, None), out_axes=1)
    own_blocks = positions.reshape(3, owned_blocks, BLK)
    own_force = fene(own_blocks, chain_order)
    total_tiles = tile_list.shape[1]
    own_force = own_force.reshape(3, -1)
    row_group = lax.all_gather(positions, "col", axis=1, tiled=True)
    column_group = lax.all_gather(positions, "row", axis=1, tiled=True)
    row_blocks = row_group.reshape(3, -1, BLK)
    column_blocks = column_group.reshape(3, -1, BLK)
    per_section = total_tiles // owned_blocks
    row_start = row_index * (column_count * owned_blocks)

    def one_section(section, totals):
        row_totals, column_totals = totals
        window = lax.dynamic_slice_in_dim(tile_list, section * per_section, per_section, 1)
        row_pick = window[0]
        column_pick = window[1]
        row_global = row_start + row_pick
        column_global = (
            column_pick // owned_blocks * column_count + column_index
        ) * owned_blocks + column_pick % owned_blocks
        same_block = row_global == column_global
        row_part, column_part = paired(
            row_blocks[:, row_pick], column_blocks[:, column_pick], same_block, periods
        )
        return (
            row_totals.at[:, row_pick].add(row_part),
            column_totals.at[:, column_pick].add(column_part),
        )

    row_totals, column_totals = lax.fori_loop(
        0, owned_blocks, one_section, (jnp.zeros_like(row_blocks), jnp.zeros_like(column_blocks))
    )
    row_force = lax.psum_scatter(row_totals.reshape(3, -1), "col", scatter_dimension=1, tiled=True)
    column_force = lax.psum_scatter(
        column_totals.reshape(3, -1), "row", scatter_dimension=1, tiled=True
    )
    forces = row_force + column_force + own_force
    new_velocity = velocities + time_step * forces
    new_position = positions + time_step * new_velocity
    return (new_velocity, new_position)


def solution(mesh):
    in_specs = (
        P(None, ("row", "col")),
        P(None, ("row", "col")),
        P(("row", "col"), None),
        P(None, ("row", "col")),
    )
    out_specs = (P(None, ("row", "col")), P(None, ("row", "col")))
    return jax.shard_map(
        on_device, mesh=mesh, in_specs=in_specs, out_specs=out_specs, check_vma=False
    )
```

profile of v0, /device:TPU:6, one launch (start us, length us, event | category | flops | bytes accessed | tf_op | source)
XLA Modules:
  0.0 564.0 jit_solution(12228082147164810531)
XLA Ops:
  7.2 53.6 %all_gather.6 = f32[3,65536]{1,0:T(4,128)S(1)} all-gather(f32[3,2048]{1,0:T(4,128)} %param.7), channel_id=1, replica_groups=mesh['row'=8,'col'=32] {'col'}, dimensions={1}, use_global_device_ids=true | all-gather | bytes 811008 | tf_op jit(solution)/shard_map/all_gather | solution.py:73
  60.8 13.0 %all_gather.7 = f32[3,16384]{1,0:T(4,128)S(1)} all-gather(f32[3,2048]{1,0:T(4,128)} %param.7), channel_id=1, replica_groups=mesh['row'=8,'col'=32] {'row'}, dimensions={1}, use_global_device_ids=true | all-gather | bytes 221184 | tf_op jit(solution)/shard_map/all_gather | solution.py:74
  74.0 99.7 %while.18 = (s32[]{:T(128)}, f32[3,512,128]{2,0,1:T(4,128)S(1)}, f32[3,128,128]{2,0,1:T(4,128)S(1)}, s32[2,80]{1,0:T(2,128)}, f32[3,512,128]{2,0,1:T(4,128)S(1)}...) while((s32[]{:T(128)}, f32[3,512,128]{2,0,1:T(4,128)S(1)}, ...), condition=%wide.region_6.7_spmd.clone, body=%wide.region_0.6_spmd.sunk.clone.sunk | while | flops 5429158 | bytes 1490529 | solution.py:98
  76.0 1.0 fusion.24
  77.4 1.3 fusion.25
  82.2 1.0 fusion.24
  83.7 1.3 fusion.25
  88.4 1.0 fusion.24
  89.9 1.3 fusion.25
  96.1 1.3 fusion.25
  102.3 1.3 fusion.25
  108.6 1.3 fusion.25
  114.8 1.3 fusion.25
  121.0 1.3 fusion.25
  127.3 1.3 fusion.25
  133.5 1.3 fusion.25
  139.8 1.3 fusion.25
  146.0 1.3 fusion.25
  152.2 1.3 fusion.25
  158.5 1.3 fusion.25
  164.7 1.3 fusion.25
  170.9 1.3 fusion.25
  173.8 4.8 copy.24
  178.7 15.6 %copy.23 = f32[3,512,128]{0,2,1:T(8,128)} copy(f32[3,512,128]{2,0,1:T(4,128)S(1)} %get-tuple-element.227) | data formatting | bytes 1572864 | tf_op jit(solution)/shard_map/while | solution.py:98
  195.3 13.0 %gather_fusion.2 = f32[2048,3]{1,0:T(8,128)S(1)} fusion(f32[3,16,128]{0,2,1:T(8,128)S(1)} %bitcast.50, s32[2048]{0:T(1024)S(1)} %or_bitcast_fusion), kind=kCustom, calls=%fused_computation.2 | custom fusion | bytes 65536 | tf_op jit(solution)/shard_map/jit(take_along_axis)/gather | solution.py:39
  209.5 1.2 pad_subtract_fusion
  210.7 6.2 %scatter_custom_fusion.2 = f32[3,2048]{0,1:T(8,128)S(1)} fusion(s32[2048]{0:T(1024)S(1)} %select_bitcast_fusion.1, f32[2048,3]{1,0:T(8,128)} %bitcast.53, f32[]{:T(128)} %constant.244.clone.1), kind=kCustom, calls=%fused_computation.46 | custom fusion | bytes 25088 | tf_op jit(solution)/shard_map/reshape | solution.py:72
  216.9 12.1 %reduce-scatter.5.cloned.1.call-done = f32[3,2048]{0,1:T(8,128)} async-done(((f32[3,16384]{0,1:T(8,128)}), f32[3,2048]{0,1:T(8,128)}) %reduce-scatter.5.cloned.1.call-update) | async-done | bytes 24592 | tf_op jit(solution)/shard_map/reduce_scatter | solution.py:102
  228.9 320.7 %reduce-scatter.3.cloned.1.call-done = f32[3,2048]{0,1:T(8,128)} async-done(((f32[3,65536]{0,1:T(8,128)}), f32[3,2048]{0,1:T(8,128)}) %reduce-scatter.3.cloned.1.call-update) | async-done | bytes 24592 | tf_op jit(solution)/shard_map/reduce_scatter | solution.py:101
  549.6 3.2 multiply_add_fusion
  552.8 2.2 copy.28
  555.0 2.2 copy.29
  (219 shorter events, 76.8 us)
Async XLA Ops:
  7.2 221.8 %reduce-scatter.5.cloned.1.call-start = ((), (), s32[]{:S(2)}) async-start(), calls=%async_computation.3 | async-start | bytes 9437184 | tf_op jit(solution)/shard_map/reduce_scatter | solution.py:102
  178.6 371.0 %reduce-scatter.3.cloned.1.call-start = ((), (), s32[]{:S(2)}) async-start(), calls=%async_computation.2 | async-start | bytes 34603008 | tf_op jit(solution)/shard_map/reduce_scatter | solution.py:101
  178.7 15.7 %copy-start.1 = (s32[16,128]{1,0:T(8,128)S(1)}, s32[16,128]{1,0:T(8,128)}, u32[]{:S(2)}) copy-start(s32[16,128]{1,0:T(8,128)} %param.9) | copy-start | bytes 24580
  178.7 15.7 %copy-start.4 = (s32[2]{0:T(128)S(1)}, s32[2]{0:T(128)}, u32[]{:S(2)}) copy-start(s32[2]{0:T(128)} %constant.267) | copy-start | bytes 28
  178.7 15.8 %copy-start.3 = (s32[2]{0:T(128)S(1)}, s32[2]{0:T(128)}, u32[]{:S(2)}) copy-start(s32[2]{0:T(128)} %constant.270) | copy-start | bytes 28
  178.7 15.9 %copy-start = (f32[3,2048]{1,0:T(4,128)S(1)}, f32[3,2048]{1,0:T(4,128)}, u32[]{:S(2)}) copy-start(f32[3,2048]{1,0:T(4,128)} %param.7) | copy-start | bytes 73732
  178.7 16.2 %copy-start.2 = (f32[3,2048]{1,0:T(4,128)S(1)}, f32[3,2048]{1,0:T(4,128)}, u32[]{:S(2)}) copy-start(f32[3,2048]{1,0:T(4,128)} %param.8) | copy-start | bytes 73732
Sparse Core Ops, SparseCore 0:
  178.8 50.1 reduce-scatter.4
  233.1 316.5 reduce-scatter.2
where the time goes:
time: 565 us; the launch traced here: 564 us
  waiting for transfers between devices  333 us (59%)
  local copies, waits for them, and re-layouts  75.3 us (13%)
  other arithmetic  74 us (13%)
  blocking collectives  66.7 us (12%)
  between operations  14.2 us (3%)
    reduce_scatter x1, waiting for transfers between devices, on_device(): lax.psum_scatter(row_totals.reshape(3, -1), 'col', scatter_dimension=1, t...  321 us
    all_gather x1, blocking collectives, on_device(): row_group = lax.all_gather(positions, 'col', axis=1, tiled=True)  53.6 us
    reduce_sum x16, other arithmetic, pair_terms(): jnp.sum(pair_force, axis=1)  21.1 us
    while x2, local copies, waits for them, and re-layouts, on_device(): lax.fori_loop(0, owned_blocks, one_section, (jnp.zeros_like(row_blocks),...  20.4 us
    reduce_sum x16, other arithmetic, pair_terms(): squared = jnp.sum(offset * offset, axis=0)  16.5 us
    gather x1, local copies, waits for them, and re-layouts, fene(): ordered = jnp.take_along_axis(block_positions, chain[None], axis=2)  13 us
    all_gather x1, blocking collectives, on_device(): column_group = lax.all_gather(positions, 'row', axis=1, tiled=True)  13 us
    dynamic_slice x16, local copies, waits for them, and re-layouts, one_section(): lax.dynamic_slice_in_dim(tile_list, section * per_section, per_section, 1)  12.1 us
  transfers between devices with their start and end apart: 2, of which 2 were waited for; matrix products, arithmetic and copies ran while one was open for 7% of the time, Pallas kernels for 0%

commit v1 on v0

v1 whole, which is shorter than its diff:
```python
import functools

import jax
import jax.numpy as jnp
from jax import lax
from jax.experimental import pallas as pl
from jax.experimental.pallas import tpu as pltpu
from jax.sharding import PartitionSpec as P

BLK = 128
CHAIN = 32
LINES_X = 4
LINES_Y = 4
OWN = 16
FAR = 64
GROUP = 8
BATCHES = FAR // GROUP
MESH = pl.DeviceIdType.MESH

cutoff = 2.5
spacing = 1.1
spring = 30.0
bond_reach = 1.5
time_step = 0.005
shift_force = 24.0 * (2.0 * cutoff ** (-13) - cutoff ** (-7))


def to_phase(x, period):
    per_unit = 2.0**32 / period
    whole = round(per_unit)
    n = jnp.floor(x)
    rest = n * jnp.float32(per_unit - whole) + (x - n) * jnp.float32(per_unit)
    return n.astype(jnp.int32) * jnp.int32(whole) + rest.astype(jnp.int32)


def pair(row, column, scales, extra=None):
    d = [(a - b).astype(jnp.float32) * s for a, b, s in zip(row, column, scales)]
    squared = d[0] * d[0] + d[1] * d[1] + d[2] * d[2]
    if extra is not None:
        squared = squared + extra
    t = lax.rsqrt(squared)
    s = t * t
    cubed = s * s * s
    magnitude = (s * cubed) * (cubed - 0.5) - jnp.float32(shift_force / 48.0) * t
    magnitude = jnp.where(squared < cutoff * cutoff, magnitude, 0.0)
    return [v * magnitude for v in d]


def skew(row, first):
    wide = jnp.broadcast_to(row, (8, BLK))
    return pltpu.roll(wide, first, 1, stride=1, stride_axis=0)


def unskew(total, first, index):
    if first:
        total = pltpu.roll(total, BLK - first, 1)
    back = jnp.take_along_axis(total, index, axis=1, mode="promise_in_bounds")
    return jnp.sum(back, axis=0, keepdims=True)


def tile(row, column, first, count, scales, extra, last_mask, index):
    row = [jnp.broadcast_to(v, (8, BLK)) for v in row]
    base = [skew(v, first) for v in column]
    to_row = to_column = None
    for r in range(count):
        now = base if r == 0 else [pltpu.roll(v, 8 * r, 1) for v in base]
        f = pair(row, now, scales, extra if r == 0 else None)
        to_row = f if to_row is None else [a + b for a, b in zip(to_row, f)]
        if last_mask is not None and r == count - 1:
            f = [jnp.where(last_mask, v, 0.0) for v in f]
        g = f if r == 0 else [pltpu.roll(v, BLK - 8 * r, 1) for v in f]
        to_column = g if to_column is None else [a + b for a, b in zip(to_column, g)]
    return (
        [jnp.sum(v, axis=0, keepdims=True) for v in to_row],
        [unskew(v, first, index) for v in to_column],
    )


def spread(one_hot, parts):
    return lax.dot_general(
        one_hot,
        parts,
        (((1,), (0,)), ((), ())),
        precision=lax.Precision.HIGHEST,
        preferred_element_type=jnp.float32,
    )


def kernel(
    NR, NY, NZ,
    tl, pos, chain, tlv, out,
    gath, colg, own_u, row_x, col_x, row_u, col_u, own_f, inv, meta, prs, cparts,
    totals, coltot, rs2, crs,
    ag_send, ag_recv, fw_send, rg_send, rg_recv, mt_send, mt_recv,
    r1_send, r1_recv, r2_send, r2_recv, rc_send, rc_recv,
):
    periods = [
        4.0 * spacing * LINES_X * NY * NZ,
        4.0 * spacing * LINES_Y * NR,
        8.0 * spacing,
    ]
    scales = [jnp.float32(v / 2.0**32) for v in periods]
    p = lax.axis_index("row")
    q = lax.axis_index("col")
    y = q // NZ
    z = q % NZ

    def at_z(d):
        return (p, y * NZ + lax.rem(z + d, NZ))

    def at_y(d):
        return (p, lax.rem(y + d, NY) * NZ + z)

    def at_row(d):
        return (lax.rem(p + d, NR), q)

    barrier = pltpu.get_barrier_semaphore()
    peers = (
        [at_z(d) for d in range(1, NZ)]
        + [at_y(d) for d in range(1, NY)]
        + [at_row(d) for d in range(1, NR)]
    )
    for peer in peers:
        pl.semaphore_signal(barrier, inc=1, device_id=peer, device_id_type=MESH)

    for d in range(3):
        for b in range(OWN):
            v = pos[d : d + 1, b * BLK : (b + 1) * BLK]
            gath[q, d, b : b + 1, :] = v
            colg[p, d, b : b + 1, :] = v
    meta[y] = jnp.full((8, BLK), -1.0, jnp.float32)
    meta[y, 0:1, 0:FAR] = tlv[0:1, OWN : OWN + FAR].astype(jnp.float32)
    pl.semaphore_wait(barrier, len(peers))

    def copy(src, dst, send, recv, peer):
        return pltpu.make_async_remote_copy(
            src_ref=src, dst_ref=dst, send_sem=send, recv_sem=recv,
            device_id=peer, device_id_type=MESH,
        )

    def z_step(i):
        half = i // 2 + 1
        return lax.rem(half + (i % 2) * (NZ - 2 * half), NZ)

    def ag_copy(d):
        return copy(gath.at[q], gath.at[q], ag_send.at[d - 1], ag_recv.at[q], at_z(d))

    def chunk_arrived(slot):
        copy(gath.at[slot], gath.at[slot], ag_send.at[0], ag_recv.at[slot], at_z(1)).wait_recv()

    def forward(slot, j, d):
        return copy(gath.at[slot], gath.at[slot], fw_send.at[j, d - 1], ag_recv.at[slot], at_y(d))

    def row_copy(d):
        return copy(colg.at[p], colg.at[p], rg_send.at[d - 1], rg_recv.at[p], at_row(d))

    def meta_copy(d):
        return copy(meta.at[y], meta.at[y], mt_send.at[d - 1], mt_recv.at[y], at_y(d))

    y_order = [1, NY - 1] + list(range(2, NY - 1)) if NY > 2 else [1]
    z_order = []
    for i in range(1, NZ):
        d = (i + 1) // 2 if i % 2 else NZ - i // 2
        z_order.append(d)
    for d in z_order[:2]:
        ag_copy(d).start()
    for d in y_order:
        forward(q, 0, d).start()
    for d in z_order[2:]:
        ag_copy(d).start()
    for d in range(1, NR):
        row_copy(d).start()
    for d in y_order:
        meta_copy(d).start()

    lane = lax.broadcasted_iota(jnp.int32, (8, BLK), 1)
    sub = lax.broadcasted_iota(jnp.int32, (8, BLK), 0)
    index = (lane + sub) & (BLK - 1)

    order = chain[...]
    x = [gath[q, d] for d in range(3)]
    for d in range(3):
        own_u[d] = to_phase(x[d], periods[d])
    order_t = jnp.transpose(order.astype(jnp.float32))
    lane_f = lax.broadcasted_iota(jnp.int32, (BLK, BLK), 1).astype(jnp.float32)
    sub_f = lax.broadcasted_iota(jnp.int32, (BLK, BLK), 0).astype(jnp.float32)
    for b in range(OWN):
        hit = order_t[:, b : b + 1] == lane_f
        inv[b : b + 1, :] = jnp.sum(jnp.where(hit, sub_f, 0.0), axis=0, keepdims=True)
    back = inv[...].astype(jnp.int32)
    ordered = [jnp.take_along_axis(v, order, axis=1, mode="promise_in_bounds") for v in x]
    bond = [pltpu.roll(v, BLK - 1, 1) - v for v in ordered]
    squared = bond[0] * bond[0] + bond[1] * bond[1] + bond[2] * bond[2]
    rank = lax.broadcasted_iota(jnp.int32, (OWN, BLK), 1) + 1
    strength = -spring / jnp.maximum(1.0 - squared / (bond_reach * bond_reach), 0.3)
    strength = jnp.where(rank % CHAIN != 0, strength, 0.0)
    for d in range(3):
        pulled = bond[d] * strength
        along = pltpu.roll(pulled, 1, 1) - pulled
        own_f[d] = jnp.take_along_axis(along, back, axis=1, mode="promise_in_bounds")

    def self_tile(k):
        u = [own_u[d, pl.ds(k, 1), :] for d in range(3)]
        to_row, to_column = tile(u, u, 1, BLK // 16, scales, None, sub < 7, index)
        for d in range(3):
            own_f[d, pl.ds(k, 1), :] += 48.0 * (to_row[d] - to_column[d])

    def self_step(i, carry):
        self_tile(2 * i)
        self_tile(2 * i + 1)
        slot = y * NZ + lax.rem(z + z_step(i), NZ)
        chunk_arrived(slot)
        for d in y_order:
            forward(slot, i + 1, d).start()
        return carry

    lax.fori_loop(0, NZ - 1, self_step, 0)

    def self_rest(i, carry):
        self_tile(2 * i)
        self_tile(2 * i + 1)
        return carry

    lax.fori_loop(NZ - 1, OWN // 2, self_rest, 0)

    def y_arrived(i, carry):
        for d in y_order:
            chunk_arrived(lax.rem(y + d, NY) * NZ + lax.rem(z + i, NZ))
        return carry

    lax.fori_loop(0, NZ, y_arrived, 0)
    for d in range(1, NR):
        slot = lax.rem(p + d, NR)
        copy(colg.at[slot], colg.at[slot], rg_send.at[0], rg_recv.at[slot], at_row(1)).wait_recv()

    def stage(i, carry):
        for j in range(GROUP):
            t = i * GROUP + j
            r = tl[0, OWN + t]
            c = tl[1, OWN + t]
            for d in range(3):
                row_x[d, pl.ds(t, 1), :] = gath[r >> 4, d, pl.ds(r & 15, 1), :]
                col_x[d, pl.ds(t, 1), :] = colg[c >> 4, d, pl.ds(c & 15, 1), :]
        return carry

    lax.fori_loop(0, BATCHES, stage, 0)

    def phase(i, carry):
        at = pl.ds(pl.multiple_of(i * GROUP, GROUP), GROUP)
        for d in range(3):
            row_u[d, at, :] = to_phase(row_x[d, at, :], periods[d])
            col_u[d, at, :] = to_phase(col_x[d, at, :], periods[d])
        return carry

    lax.fori_loop(0, BATCHES, phase, 0)

    def far_tile(b, j):
        t = b * GROUP + j
        r = tl[0, OWN + t]
        c = tl[1, OWN + t]
        same = p * (NY * NZ * OWN) + r == ((c >> 4) * (NY * NZ) + q) * OWN + (c & 15)
        extra = jnp.where((sub == 0) & same, 1e6, 0.0)
        u = [row_u[d, pl.ds(t, 1), :] for d in range(3)]
        v = [col_u[d, pl.ds(t, 1), :] for d in range(3)]
        to_row, to_column = tile(u, v, 0, BLK // 8, scales, extra, None, index)
        for d in range(3):
            prs[y, b, d, pl.ds(j, 1), :] = to_row[d]
            cparts[b, d, pl.ds(j, 1), :] = to_column[d]

    def r1_copy(b, d):
        return copy(
            prs.at[y, b], prs.at[y, b], r1_send.at[b, d - 1], r1_recv.at[y, b], at_y(d)
        )

    def batch(b, carry):
        def two(j, inner):
            far_tile(b, 2 * j)
            far_tile(b, 2 * j + 1)
            return inner

        lax.fori_loop(0, GROUP // 2, two, 0)
        for d in y_order:
            r1_copy(b, d).start()
        return carry

    lax.fori_loop(0, BATCHES, batch, 0)

    r = tlv[0:1, OWN : OWN + FAR]
    c = tlv[1:2, OWN : OWN + FAR]
    same = p * (NY * NZ * OWN) + r == ((c >> 4) * (NY * NZ) + q) * OWN + (c & 15)
    rows = lax.broadcasted_iota(jnp.int32, (NR * OWN, FAR), 0)
    minus = jnp.where((rows == c) & jnp.logical_not(same), -1.0, 0.0)
    for d in range(3):
        full = spread(minus, cparts[:, d].reshape(FAR, BLK))
        coltot[:, d] = full.reshape(NR, OWN, BLK)

    def rc_copy(d):
        to = lax.rem(p + d, NR)
        return copy(coltot.at[to], crs.at[p], rc_send.at[d - 1], rc_recv.at[p], at_row(d))

    for d in range(1, NR):
        rc_copy(d).start()

    for d in y_order:
        slot = lax.rem(y + d, NY)
        copy(meta.at[slot], meta.at[slot], mt_send.at[0], mt_recv.at[slot], at_y(1)).wait_recv()

    def r1_arrived(b, carry):
        for d in y_order:
            slot = lax.rem(y + d, NY)
            copy(
                prs.at[slot, b], prs.at[slot, b], r1_send.at[0, 0], r1_recv.at[slot, b], at_y(1)
            ).wait_recv()
        return carry

    lax.fori_loop(0, BATCHES, r1_arrived, 0)
    names = jnp.concatenate([meta[i, 0:1, 0:FAR] for i in range(NY)], axis=1)
    mine = lax.broadcasted_iota(jnp.int32, (NZ * OWN, NY * FAR), 0) + y * (NZ * OWN)
    plus = jnp.where(mine.astype(jnp.float32) == names, 1.0, 0.0)
    for d in range(3):
        full = spread(plus, prs[:, :, d].reshape(NY * FAR, BLK))
        totals[:, d] = full.reshape(NZ, OWN, BLK)

    def r2_copy(d):
        to = lax.rem(z + d, NZ)
        return copy(totals.at[to], rs2.at[z], r2_send.at[d - 1], r2_recv.at[z], at_z(d))

    for d in reversed(z_order):
        r2_copy(d).start()

    acc = [coltot[p, d] for d in range(3)]
    for i in range(1, NR):
        slot = lax.rem(p + i, NR)
        copy(coltot.at[slot], crs.at[slot], rc_send.at[0], rc_recv.at[slot], at_row(1)).wait_recv()
        acc = [acc[d] + crs[slot, d] for d in range(3)]
    acc = [acc[d] + totals[z, d] for d in range(3)]
    for i in z_order:
        slot = lax.rem(z + i, NZ)
        copy(totals.at[slot], rs2.at[slot], r2_send.at[0], r2_recv.at[slot], at_z(1)).wait_recv()
        acc = [acc[d] + rs2[slot, d] for d in range(3)]
    for d in range(3):
        total = 48.0 * acc[d] + own_f[d]
        for b in range(OWN):
            out[d : d + 1, b * BLK : (b + 1) * BLK] = total[b : b + 1, :]

    for d in range(1, NZ):
        ag_copy(d).wait_send()
        r2_copy(d).wait_send()
    for d in range(1, NR):
        row_copy(d).wait_send()
        rc_copy(d).wait_send()
    for d in range(1, NY):
        meta_copy(d).wait_send()

    def left(i, carry):
        for d in range(1, NY):
            forward(q, i, d).wait_send()
        return carry

    lax.fori_loop(0, NZ, left, 0)

    def left_parts(b, carry):
        for d in range(1, NY):
            r1_copy(b, d).wait_send()
        return carry

    lax.fori_loop(0, BATCHES, left_parts, 0)


def on_device(NR, NY, NZ, positions, velocities, chain_order, tile_list):
    f32 = jnp.float32
    dma = pltpu.SemaphoreType.DMA
    vmem = pl.BlockSpec(memory_space=pltpu.VMEM)
    forces = pl.pallas_call(
        functools.partial(kernel, NR, NY, NZ),
        out_shape=jax.ShapeDtypeStruct(positions.shape, f32),
        in_specs=[pl.BlockSpec(memory_space=pltpu.SMEM), vmem, vmem, vmem],
        out_specs=vmem,
        scratch_shapes=[
            pltpu.VMEM((NY * NZ, 3, OWN, BLK), f32),
            pltpu.VMEM((NR, 3, OWN, BLK), f32),
            pltpu.VMEM((3, OWN, BLK), jnp.int32),
            pltpu.VMEM((3, FAR, BLK), f32),
            pltpu.VMEM((3, FAR, BLK), f32),
            pltpu.VMEM((3, FAR, BLK), jnp.int32),
            pltpu.VMEM((3, FAR, BLK), jnp.int32),
            pltpu.VMEM((3, OWN, BLK), f32),
            pltpu.VMEM((OWN, BLK), f32),
            pltpu.VMEM((NY, 8, BLK), f32),
            pltpu.VMEM((NY, BATCHES, 3, GROUP, BLK), f32),
            pltpu.VMEM((BATCHES, 3, GROUP, BLK), f32),
            pltpu.VMEM((NZ, 3, OWN, BLK), f32),
            pltpu.VMEM((NR, 3, OWN, BLK), f32),
            pltpu.VMEM((NZ, 3, OWN, BLK), f32),
            pltpu.VMEM((NR, 3, OWN, BLK), f32),
            dma((NZ - 1,)),
            dma((NY * NZ,)),
            dma((NZ, NY - 1)),
            dma((NR - 1,)),
            dma((NR,)),
            dma((NY - 1,)),
            dma((NY,)),
            dma((BATCHES, NY - 1)),
            dma((NY, BATCHES)),
            dma((NZ - 1,)),
            dma((NZ,)),
            dma((NR - 1,)),
            dma((NR,)),
        ],
        compiler_params=pltpu.CompilerParams(
            collective_id=0, has_side_effects=True, vmem_limit_bytes=32 * 1024 * 1024
        ),
    )(tile_list, positions, chain_order, tile_list)
    new_velocity = velocities + time_step * forces
    new_position = positions + time_step * new_velocity
    return (new_velocity, new_position)


def solution(mesh, NZ=8):
    in_specs = (
        P(None, ("row", "col")),
        P(None, ("row", "col")),
        P(("row", "col"), None),
        P(None, ("row", "col")),
    )
    out_specs = (P(None, ("row", "col")), P(None, ("row", "col")))
    return jax.shard_map(
        functools.partial(on_device, mesh.shape["row"], mesh.shape["col"] // NZ, NZ),
        mesh=mesh,
        in_specs=in_specs,
        out_specs=out_specs,
        check_vma=False,
    )
```

time: 565 us -> 50.2 us (0.09)
  waiting for transfers between devices: 333 us -> 0 us
  other arithmetic: 74 us -> 0.65 us
  local copies, waits for them, and re-layouts: 75.3 us -> 2.13 us
  blocking collectives: 66.7 us -> 0 us
  Pallas kernels: 0 us -> 46.4 us
  between operations: 14.2 us -> 0.66 us
    reduce_scatter x2 -> x0, waiting for transfers between devices: 333 us -> none  [the longest x1 321 us: on_device(): lax.psum_scatter(row_totals.reshape(3, -1), 'col', scatter_dimension=1, t...]
    all_gather x2 -> x0, blocking collectives: 66.7 us -> none  [the longest x1 53.6 us: on_device(): row_group = lax.all_gather(positions, 'col', axis=1, tiled=True)]
    pallas_call x0 -> x1, Pallas kernels: none -> 46.4 us  [on_device(): pl.pallas_call(functools.partial(kernel, NR, NY, NZ), out_shape=jax.Shape...]
    reduce_sum x33 -> x0, other arithmetic: 37.9 us -> none  [the longest x16 21.1 us: pair_terms(): jnp.sum(pair_force, axis=1)]
    gather x33 -> x0, local copies, waits for them, and re-layouts: 31.3 us -> none  [the longest x1 13 us: fene(): ordered = jnp.take_along_axis(block_positions, chain[None], axis=2)]
    scatter-add x32 -> x0, other arithmetic: 23.2 us -> none  [the longest x16 11.6 us: one_section(): row_totals.at[:, row_pick].add(row_part)]
    while x2 -> x0, local copies, waits for them, and re-layouts: 20.4 us -> none  [on_device(): lax.fori_loop(0, owned_blocks, one_section, (jnp.zeros_like(row_blocks),...]
    dynamic_slice x16 -> x0, local copies, waits for them, and re-layouts: 12.1 us -> none  [one_section(): lax.dynamic_slice_in_dim(tile_list, section * per_section, per_section, 1)]
  transfers between devices with their start and end apart: 2 -> 0, of which waited for: 2 -> 0; matrix products, arithmetic and copies ran while one was open for 7% -> 0% of each run, Pallas kernels for 0% -> 0%
where the time goes in v1:
time: 50.2 us; the launch traced here: 49.8 us
  Pallas kernels  46.4 us (92%)
  local copies, waits for them, and re-layouts  2.13 us (4%)
  between operations  0.66 us (1%)
  other arithmetic  0.65 us (1%)
    pallas_call x1, Pallas kernels, on_device(): pl.pallas_call(functools.partial(kernel, NR, NY, NZ), out_shape=jax.Shape...  46.4 us
    unnamed x8, local copies, waits for them, and re-layouts  2.13 us

profile of v1, /device:TPU:6, one launch (start us, length us, event | category | flops | bytes accessed | tf_op | source)
XLA Modules:
  0.0 49.8 jit_solution(14952767125942587357)
XLA Ops:
  0.6 0.0 copy-start
  0.6 0.7 %copy-done = f32[3,2048]{1,0:T(4,128)S(1)} copy-done((f32[3,2048]{1,0:T(4,128)S(1)}, f32[3,2048]{1,0:T(4,128)}, u32[]{:S(2)}) %copy-start) | copy-done | bytes 24600
  1.4 0.0 copy-start.1
  1.4 0.7 %copy-done.1 = s32[16,128]{1,0:T(8,128)S(1)} copy-done((s32[16,128]{1,0:T(8,128)S(1)}, s32[16,128]{1,0:T(8,128)}, u32[]{:S(2)}) %copy-start.1) | copy-done | bytes 8216
  2.1 0.0 copy-start.2
  2.1 0.7 %copy-done.2 = s32[2,80]{1,0:T(2,128)S(1)} copy-done((s32[2,80]{1,0:T(2,128)S(1)}, s32[2,80]{1,0:T(2,128)}, u32[]{:S(2)}) %copy-start.2) | copy-done | bytes 664
  2.8 0.0 copy-start.3
  2.8 46.4 %shard_map.59 = f32[3,2048]{1,0:T(4,128)S(1)} custom-call(s32[2,80]{1,0:T(2,128)S(1)} %copy-done.2, f32[3,2048]{1,0:T(4,128)S(1)} %copy-done, s32[16,128]{1,0:T(8,128)S(1)} %copy-done.1, s32[2,80]{1,0:T(2,128)S(1)} %copy-done.2), custom_call_target="tpu_custom_call" | custom-call | tf_op jit(solution)/shard_map/pallas_call | solution.py:374
  49.2 0.0 copy-done.3
  49.2 0.6 %multiply_add_fusion = (f32[3,2048]{1,0:T(4,128)}, f32[3,2048]{1,0:T(4,128)}) fusion(f32[3,2048]{1,0:T(4,128)S(1)} %copy-done, f32[3,2048]{1,0:T(4,128)S(1)} %copy-done.3, f32[3,2048]{1,0:T(4,128)S(1)} %shard_map.59), kind=kLoop, calls=%fused_computation | loop fusion | flops 24576 | bytes 122880 | tf_op jit(solution)/shard_map/add | solution.py:415
Async XLA Ops:
  0.6 0.8 %copy-start = (f32[3,2048]{1,0:T(4,128)S(1)}, f32[3,2048]{1,0:T(4,128)}, u32[]{:S(2)}) copy-start(f32[3,2048]{1,0:T(4,128)} %pos.1) | copy-start | bytes 73732
  1.4 0.7 %copy-start.1 = (s32[16,128]{1,0:T(8,128)S(1)}, s32[16,128]{1,0:T(8,128)}, u32[]{:S(2)}) copy-start(s32[16,128]{1,0:T(8,128)} %chain.1) | copy-start | bytes 24580
  2.1 0.7 %copy-start.2 = (s32[2,80]{1,0:T(2,128)S(1)}, s32[2,80]{1,0:T(2,128)}, u32[]{:S(2)}) copy-start(s32[2,80]{1,0:T(2,128)} %tlv.1) | copy-start | bytes 1924
  2.8 46.4 %copy-start.3 = (f32[3,2048]{1,0:T(4,128)S(1)}, f32[3,2048]{1,0:T(4,128)}, u32[]{:S(2)}) copy-start(f32[3,2048]{1,0:T(4,128)} %param.5) | copy-start | bytes 73732

commit v2 on v1

--- a/solution.py
+++ b/solution.py
@@ -23,6 +23,9 @@
 bond_reach = 1.5
 time_step = 0.005
 shift_force = 24.0 * (2.0 * cutoff ** (-13) - cutoff ** (-7))
+strength = -shift_force
+unit = (48.0 / strength) ** (1.0 / 13.0)
+middle = 0.5 * unit**6
 
 
 def to_phase(x, period):
@@ -41,8 +44,8 @@
     t = lax.rsqrt(squared)
     s = t * t
     cubed = s * s * s
-    magnitude = (s * cubed) * (cubed - 0.5) - jnp.float32(shift_force / 48.0) * t
-    magnitude = jnp.where(squared < cutoff * cutoff, magnitude, 0.0)
+    magnitude = (s * cubed) * (cubed - jnp.float32(middle)) + t
+    magnitude = jnp.where(squared < jnp.float32((cutoff / unit) ** 2), magnitude, 0.0)
     return [v * magnitude for v in d]
 
 
@@ -51,29 +54,44 @@
     return pltpu.roll(wide, first, 1, stride=1, stride_axis=0)
 
 
-def unskew(total, first, index):
-    if first:
-        total = pltpu.roll(total, BLK - first, 1)
-    back = jnp.take_along_axis(total, index, axis=1, mode="promise_in_bounds")
-    return jnp.sum(back, axis=0, keepdims=True)
-
-
-def tile(row, column, first, count, scales, extra, last_mask, index):
-    row = [jnp.broadcast_to(v, (8, BLK)) for v in row]
-    base = [skew(v, first) for v in column]
-    to_row = to_column = None
-    for r in range(count):
-        now = base if r == 0 else [pltpu.roll(v, 8 * r, 1) for v in base]
-        f = pair(row, now, scales, extra if r == 0 else None)
-        to_row = f if to_row is None else [a + b for a, b in zip(to_row, f)]
-        if last_mask is not None and r == count - 1:
-            f = [jnp.where(last_mask, v, 0.0) for v in f]
-        g = f if r == 0 else [pltpu.roll(v, BLK - 8 * r, 1) for v in f]
-        to_column = g if to_column is None else [a + b for a, b in zip(to_column, g)]
-    return (
-        [jnp.sum(v, axis=0, keepdims=True) for v in to_row],
-        [unskew(v, first, index) for v in to_column],
-    )
+def meet(rows, columns, scales, extra, last_mask):
+    to_rows = [None] * len(rows)
+    to_columns = [None] * len(columns)
+    for i, row in enumerate(rows):
+        for j, column in enumerate(columns):
+            f = pair(row, column, scales, extra if i + j == 0 else None)
+            to_rows[i] = f if j == 0 else [x + v for x, v in zip(to_rows[i], f)]
+            if last_mask is not None and (i, j) == (len(rows) - 1, len(columns) - 1):
+                f = [jnp.where(last_mask, v, 0.0) for v in f]
+            to_columns[j] = f if i == 0 else [x + v for x, v in zip(to_columns[j], f)]
+    return to_rows, to_columns
+
+
+def settle_row(parts):
+    total = parts[0]
+    for i, v in enumerate(parts[1:], 1):
+        total = total + pltpu.roll(v, 8 * i, 1)
+    return total
+
+
+def settle_column(parts, shifts):
+    total = None
+    for v, shift in zip(parts, shifts):
+        v = pltpu.roll(v, BLK - shift, 1) if shift else v
+        total = v if total is None else total + v
+    return total
+
+
+def unskew(total, index):
+    return jnp.take_along_axis(total, index, axis=1, mode="promise_in_bounds")
+
+
+def fold(total):
+    return jnp.sum(total, axis=0, keepdims=True)
+
+
+FAR_SHIFTS = (0, 32, 64, 96)
+SELF_SHIFTS = (1, 17, 33, 49)
 
 
 def spread(one_hot, parts):
@@ -89,7 +107,7 @@
 def kernel(
     NR, NY, NZ,
     tl, pos, chain, tlv, out,
-    gath, colg, own_u, row_x, col_x, row_u, col_u, own_f, inv, meta, prs, cparts,
+    gath, colg, own_u, row_x, col_x, row_u, col_u, skewed, held, rolled, own_f, inv, meta, prs, cparts,
     totals, coltot, rs2, crs,
     ag_send, ag_recv, fw_send, rg_send, rg_recv, mt_send, mt_recv,
     r1_send, r1_recv, r2_send, r2_recv, rc_send, rc_recv,
@@ -99,7 +117,7 @@
         4.0 * spacing * LINES_Y * NR,
         8.0 * spacing,
     ]
-    scales = [jnp.float32(v / 2.0**32) for v in periods]
+    scales = [jnp.float32(v / 2.0**32 / unit) for v in periods]
     p = lax.axis_index("row")
     q = lax.axis_index("col")
     y = q // NZ
@@ -192,18 +210,23 @@
     bond = [pltpu.roll(v, BLK - 1, 1) - v for v in ordered]
     squared = bond[0] * bond[0] + bond[1] * bond[1] + bond[2] * bond[2]
     rank = lax.broadcasted_iota(jnp.int32, (OWN, BLK), 1) + 1
-    strength = -spring / jnp.maximum(1.0 - squared / (bond_reach * bond_reach), 0.3)
-    strength = jnp.where(rank % CHAIN != 0, strength, 0.0)
-    for d in range(3):
-        pulled = bond[d] * strength
+    stiffness = -spring / jnp.maximum(1.0 - squared / (bond_reach * bond_reach), 0.3)
+    stiffness = jnp.where(rank % CHAIN != 0, stiffness, 0.0)
+    for d in range(3):
+        pulled = bond[d] * stiffness
         along = pltpu.roll(pulled, 1, 1) - pulled
         own_f[d] = jnp.take_along_axis(along, back, axis=1, mode="promise_in_bounds")
 
     def self_tile(k):
         u = [own_u[d, pl.ds(k, 1), :] for d in range(3)]
-        to_row, to_column = tile(u, u, 1, BLK // 16, scales, None, sub < 7, index)
+        wide = [jnp.broadcast_to(v, (8, BLK)) for v in u]
+        rows = [wide, [pltpu.roll(v, BLK - 8, 1) for v in wide]]
+        columns = [[skew(v, shift) for v in u] for shift in SELF_SHIFTS]
+        to_rows, to_columns = meet(rows, columns, scales, None, sub < 7)
         for d in range(3):
-            own_f[d, pl.ds(k, 1), :] += 48.0 * (to_row[d] - to_column[d])
+            force = settle_row([v[d] for v in to_rows])
+            force -= unskew(settle_column([v[d] for v in to_columns], SELF_SHIFTS), index)
+            own_f[d, pl.ds(k, 1), :] += strength * fold(force)
 
     def self_step(i, carry):
         self_tile(2 * i)
@@ -248,42 +271,68 @@
     def phase(i, carry):
         at = pl.ds(pl.multiple_of(i * GROUP, GROUP), GROUP)
         for d in range(3):
-            row_u[d, at, :] = to_phase(row_x[d, at, :], periods[d])
+            u = to_phase(row_x[d, at, :], periods[d])
+            row_u[0, d, at, :] = u
+            for k in range(1, 4):
+                row_u[k, d, at, :] = pltpu.roll(u, BLK - 8 * k, 1)
             col_u[d, at, :] = to_phase(col_x[d, at, :], periods[d])
         return carry
 
     lax.fori_loop(0, BATCHES, phase, 0)
 
-    def far_tile(b, j):
-        t = b * GROUP + j
-        r = tl[0, OWN + t]
-        c = tl[1, OWN + t]
-        same = p * (NY * NZ * OWN) + r == ((c >> 4) * (NY * NZ) + q) * OWN + (c & 15)
-        extra = jnp.where((sub == 0) & same, 1e6, 0.0)
-        u = [row_u[d, pl.ds(t, 1), :] for d in range(3)]
-        v = [col_u[d, pl.ds(t, 1), :] for d in range(3)]
-        to_row, to_column = tile(u, v, 0, BLK // 8, scales, extra, None, index)
+    def head(t):
         for d in range(3):
-            prs[y, b, d, pl.ds(j, 1), :] = to_row[d]
-            cparts[b, d, pl.ds(j, 1), :] = to_column[d]
+            u = col_u[d, pl.ds(t, 1), :]
+            for k, shift in enumerate(FAR_SHIFTS):
+                skewed[k, d] = skew(u, shift)
 
     def r1_copy(b, d):
         return copy(
             prs.at[y, b], prs.at[y, b], r1_send.at[b, d - 1], r1_recv.at[y, b], at_y(d)
         )
 
+    def far_step(t, carry):
+        before = jnp.maximum(t - 2, 0)
+        for d in range(3):
+            at = pl.ds(before % GROUP, 1)
+            prs[y, before // GROUP, d, at, :] = fold(rolled[d])
+            cparts[before // GROUP, d, at, :] = fold(unskew(rolled[3 + d], index))
+        for d in range(3):
+            rolled[d] = settle_row([held[k, d] for k in range(4)])
+            rolled[3 + d] = settle_column([held[4 + k, d] for k in range(4)], FAR_SHIFTS)
+        now = jnp.minimum(t, FAR - 1)
+        r = tl[0, OWN + now]
+        c = tl[1, OWN + now]
+        same = p * (NY * NZ * OWN) + r == ((c >> 4) * (NY * NZ) + q) * OWN + (c & 15)
+        extra = jnp.where((sub == 0) & same, 1e6, 0.0)
+        rows = [
+            [jnp.broadcast_to(row_u[k, d, pl.ds(now, 1), :], (8, BLK)) for d in range(3)]
+            for k in range(4)
+        ]
+        columns = [[skewed[k, d] for d in range(3)] for k in range(4)]
+        to_rows, to_columns = meet(rows, columns, scales, extra, None)
+        head(jnp.minimum(t + 1, FAR - 1))
+        for k in range(4):
+            for d in range(3):
+                held[k, d] = to_rows[k][d]
+                held[4 + k, d] = to_columns[k][d]
+        return carry
+
     def batch(b, carry):
-        def two(j, inner):
-            far_tile(b, 2 * j)
-            far_tile(b, 2 * j + 1)
-            return inner
-
-        lax.fori_loop(0, GROUP // 2, two, 0)
-        for d in y_order:
-            r1_copy(b, d).start()
-        return carry
-
-    lax.fori_loop(0, BATCHES, batch, 0)
+        start = b * GROUP
+        lax.fori_loop(start, start + jnp.where(b < BATCHES, GROUP, 2), far_step, 0)
+
+        @pl.when(b > 0)
+        def _():
+            for d in y_order:
+                r1_copy(b - 1, d).start()
+
+        return carry
+
+    held[...] = jnp.zeros_like(held)
+    rolled[...] = jnp.zeros_like(rolled)
+    head(0)
+    lax.fori_loop(0, BATCHES + 1, batch, 0)
 
     r = tlv[0:1, OWN : OWN + FAR]
     c = tlv[1:2, OWN : OWN + FAR]
@@ -339,7 +388,7 @@
         copy(totals.at[slot], rs2.at[slot], r2_send.at[0], r2_recv.at[slot], at_z(1)).wait_recv()
         acc = [acc[d] + rs2[slot, d] for d in range(3)]
     for d in range(3):
-        total = 48.0 * acc[d] + own_f[d]
+        total = strength * acc[d] + own_f[d]
         for b in range(OWN):
             out[d : d + 1, b * BLK : (b + 1) * BLK] = total[b : b + 1, :]
 
@@ -382,8 +431,11 @@
             pltpu.VMEM((3, OWN, BLK), jnp.int32),
             pltpu.VMEM((3, FAR, BLK), f32),
             pltpu.VMEM((3, FAR, BLK), f32),
+            pltpu.VMEM((4, 3, FAR, BLK), jnp.int32),
             pltpu.VMEM((3, FAR, BLK), jnp.int32),
-            pltpu.VMEM((3, FAR, BLK), jnp.int32),
+            pltpu.VMEM((4, 3, 8, BLK), jnp.int32),
+            pltpu.VMEM((8, 3, 8, BLK), f32),
+            pltpu.VMEM((6, 8, BLK), f32),
             pltpu.VMEM((3, OWN, BLK), f32),
             pltpu.VMEM((OWN, BLK), f32),
             pltpu.VMEM((NY, 8, BLK), f32),

time: 50.2 us -> 44 us (0.88)
  Pallas kernels: 46.4 us -> 40.2 us
    pallas_call x1, Pallas kernels: 46.4 us -> 40.2 us  [on_device(): pl.pallas_call(functools.partial(kernel, NR, NY, NZ), out_shape=jax.Shape...]
where the time goes in v2:
time: 44 us; the launch traced here: 43.6 us
  Pallas kernels  40.2 us (91%)
  local copies, waits for them, and re-layouts  2.13 us (5%)
  between operations  0.66 us (2%)
  other arithmetic  0.65 us (1%)
    pallas_call x1, Pallas kernels, on_device(): pl.pallas_call(functools.partial(kernel, NR, NY, NZ), out_shape=jax.Shape...  40.2 us
    unnamed x8, local copies, waits for them, and re-layouts  2.13 us

profile of v2, /device:TPU:6, one launch (start us, length us, event | category | flops | bytes accessed | tf_op | source)
XLA Modules:
  0.0 43.6 jit_solution(14038614126034842205)
XLA Ops:
  0.6 0.0 copy-start
  0.6 0.7 %copy-done = f32[3,2048]{1,0:T(4,128)S(1)} copy-done((f32[3,2048]{1,0:T(4,128)S(1)}, f32[3,2048]{1,0:T(4,128)}, u32[]{:S(2)}) %copy-start) | copy-done | bytes 24600
  1.4 0.0 copy-start.1
  1.4 0.7 %copy-done.1 = s32[16,128]{1,0:T(8,128)S(1)} copy-done((s32[16,128]{1,0:T(8,128)S(1)}, s32[16,128]{1,0:T(8,128)}, u32[]{:S(2)}) %copy-start.1) | copy-done | bytes 8216
  2.1 0.0 copy-start.2
  2.1 0.7 %copy-done.2 = s32[2,80]{1,0:T(2,128)S(1)} copy-done((s32[2,80]{1,0:T(2,128)S(1)}, s32[2,80]{1,0:T(2,128)}, u32[]{:S(2)}) %copy-start.2) | copy-done | bytes 664
  2.8 0.0 copy-start.3
  2.8 40.2 %shard_map.59 = f32[3,2048]{1,0:T(4,128)S(1)} custom-call(s32[2,80]{1,0:T(2,128)S(1)} %copy-done.2, f32[3,2048]{1,0:T(4,128)S(1)} %copy-done, s32[16,128]{1,0:T(8,128)S(1)} %copy-done.1, s32[2,80]{1,0:T(2,128)S(1)} %copy-done.2), custom_call_target="tpu_custom_call" | custom-call | tf_op jit(solution)/shard_map/pallas_call | solution.py:423
  43.0 0.0 copy-done.3
  43.0 0.6 %multiply_add_fusion = (f32[3,2048]{1,0:T(4,128)}, f32[3,2048]{1,0:T(4,128)}) fusion(f32[3,2048]{1,0:T(4,128)S(1)} %copy-done, f32[3,2048]{1,0:T(4,128)S(1)} %copy-done.3, f32[3,2048]{1,0:T(4,128)S(1)} %shard_map.59), kind=kLoop, calls=%fused_computation | loop fusion | flops 24576 | bytes 122880 | tf_op jit(solution)/shard_map/add | solution.py:467
Async XLA Ops:
  0.6 0.8 %copy-start = (f32[3,2048]{1,0:T(4,128)S(1)}, f32[3,2048]{1,0:T(4,128)}, u32[]{:S(2)}) copy-start(f32[3,2048]{1,0:T(4,128)} %pos.1) | copy-start | bytes 73732
  1.4 0.7 %copy-start.1 = (s32[16,128]{1,0:T(8,128)S(1)}, s32[16,128]{1,0:T(8,128)}, u32[]{:S(2)}) copy-start(s32[16,128]{1,0:T(8,128)} %chain.1) | copy-start | bytes 24580
  2.1 0.7 %copy-start.2 = (s32[2,80]{1,0:T(2,128)S(1)}, s32[2,80]{1,0:T(2,128)}, u32[]{:S(2)}) copy-start(s32[2,80]{1,0:T(2,128)} %tlv.1) | copy-start | bytes 1924
  2.8 40.2 %copy-start.3 = (f32[3,2048]{1,0:T(4,128)S(1)}, f32[3,2048]{1,0:T(4,128)}, u32[]{:S(2)}) copy-start(f32[3,2048]{1,0:T(4,128)} %param.5) | copy-start | bytes 73732

commit v3 on v0

v3 whole, which is shorter than its diff:
```python
import functools

import jax
import jax.numpy as jnp
from jax import lax
from jax.experimental import pallas as pl
from jax.experimental.pallas import tpu as pltpu
from jax.sharding import PartitionSpec as P

BLK = 128
CHAIN = 32
LINES_X = 4
LINES_Y = 4
OWN = 16
FAR = 64
GROUP = 8
BATCHES = FAR // GROUP
MESH = pl.DeviceIdType.MESH

cutoff = 2.5
spacing = 1.1
spring = 30.0
bond_reach = 1.5
time_step = 0.005
shift_force = 24.0 * (2.0 * cutoff ** (-13) - cutoff ** (-7))
strength = -shift_force
unit = (48.0 / strength) ** (1.0 / 13.0)
middle = 0.5 * unit**6


def to_phase(x, period):
    per_unit = 2.0**32 / period
    whole = round(per_unit)
    n = jnp.floor(x)
    rest = n * jnp.float32(per_unit - whole) + (x - n) * jnp.float32(per_unit)
    return n.astype(jnp.int32) * jnp.int32(whole) + rest.astype(jnp.int32)


def pair(row, column, scales, extra=None):
    d = [(a - b).astype(jnp.float32) * s for a, b, s in zip(row, column, scales)]
    squared = d[0] * d[0] + d[1] * d[1] + d[2] * d[2]
    if extra is not None:
        squared = squared + extra
    t = lax.rsqrt(squared)
    s = t * t
    cubed = s * s * s
    magnitude = (s * cubed) * (cubed - jnp.float32(middle)) + t
    magnitude = jnp.where(squared < jnp.float32((cutoff / unit) ** 2), magnitude, 0.0)
    return [v * magnitude for v in d]


def skew(row, first):
    wide = jnp.broadcast_to(row, (8, BLK))
    return pltpu.roll(wide, first, 1, stride=1, stride_axis=0)


def meet(rows, columns, scales, extra, last_mask):
    to_rows = [None] * len(rows)
    to_columns = [None] * len(columns)
    for i, row in enumerate(rows):
        for j, column in enumerate(columns):
            f = pair(row, column, scales, extra if i + j == 0 else None)
            to_rows[i] = f if j == 0 else [x + v for x, v in zip(to_rows[i], f)]
            if last_mask is not None and (i, j) == (len(rows) - 1, len(columns) - 1):
                f = [jnp.where(last_mask, v, 0.0) for v in f]
            to_columns[j] = f if i == 0 else [x + v for x, v in zip(to_columns[j], f)]
    return to_rows, to_columns


def settle_row(parts):
    total = parts[0]
    for i, v in enumerate(parts[1:], 1):
        total = total + pltpu.roll(v, 8 * i, 1)
    return total


def settle_column(parts, shifts):
    total = None
    for v, shift in zip(parts, shifts):
        v = pltpu.roll(v, BLK - shift, 1) if shift else v
        total = v if total is None else total + v
    return total


def unskew(total, index):
    return jnp.take_along_axis(total, index, axis=1, mode="promise_in_bounds")


def fold(total):
    return jnp.sum(total, axis=0, keepdims=True)


FAR_SHIFTS = (0, 32, 64, 96)
SELF_SHIFTS = (1, 17, 33, 49)


def spread(one_hot, parts):
    total = None
    for _ in range(3):
        piece = parts.astype(jnp.bfloat16)
        parts = parts - piece.astype(jnp.float32)
        product = jnp.dot(one_hot, piece, preferred_element_type=jnp.float32)
        total = product if total is None else total + product
    return total


def kernel(
    NR, NY, NZ,
    tl_any, pos_any, chain_any, out,
    tl, tlv, pos, chain, gath, colg, gath_u, colg_u, rowed, skewed, held, rolled,
    own_f, inv, meta, prs, cparts, totals, coltot, rs2, crs,
    in_sem, sent, a_recv, b_recv, group_recv, r1_recv,
):
    periods = [
        4.0 * spacing * LINES_X * NY * NZ,
        4.0 * spacing * LINES_Y * NR,
        8.0 * spacing,
    ]
    scales = [jnp.float32(v / 2.0**32 / unit) for v in periods]
    p = lax.axis_index("row")
    q = lax.axis_index("col")
    y = q >> (NZ.bit_length() - 1)
    z = q & (NZ - 1)

    def at_z(d):
        return (p, y * NZ + ((z + d) & (NZ - 1)))

    def at_y(d):
        return (p, ((y + d) & (NY - 1)) * NZ + z)

    def at_row(d):
        return ((p + d) & (NR - 1), q)

    barrier = pltpu.get_barrier_semaphore()
    peers = (
        [at_z(d) for d in sorted(range(1, NZ), key=lambda d: -min(d, NZ - d))]
        + [at_y(d) for d in range(1, NY)]
        + [at_row(d) for d in range(1, NR)]
    )
    for peer in peers:
        pl.semaphore_signal(barrier, inc=1, device_id=peer, device_id_type=MESH)
    reads = [
        pltpu.make_async_copy(src, dst, in_sem.at[i])
        for i, (src, dst) in enumerate(
            [(pos_any, pos), (chain_any, chain), (tl_any, tl), (tl_any, tlv)]
        )
    ]
    for read in reads:
        read.start()

    y_order = [1, NY - 1] + list(range(2, NY - 1)) if NY > 2 else [1]
    z_order = [(i + 1) // 2 if i % 2 else NZ - i // 2 for i in range(1, NZ)]

    def copy(src, dst, send, recv, peer):
        return pltpu.make_async_remote_copy(
            src_ref=src, dst_ref=dst, send_sem=send, recv_sem=recv,
            device_id=peer, device_id_type=MESH,
        )

    def arrived(sem, like):
        pltpu.make_async_copy(like, like, sem).wait()

    def slot_of(u, v):
        return ((y + u) & (NY - 1)) * NZ + ((z + v) & (NZ - 1))

    def a_part(slot, send, recv, peer):
        ref = gath.at[slot, pl.ds(0, 2)]
        return copy(ref, ref, send, recv, peer)

    def b_part(slot, send, recv, peer):
        ref = gath.at[slot, 2]
        return copy(ref, ref, send, recv, peer)

    def a_first(d):
        return a_part(q, sent.at[0], a_recv.at[0, z], at_z(d))

    def a_then(k, d):
        far_z = (z + k) & (NZ - 1)
        return a_part(y * NZ + far_z, sent.at[1], a_recv.at[1, far_z], at_y(d))

    def b_first(d):
        return b_part(q, sent.at[2], b_recv.at[0, y], at_y(d))

    def b_then(k, d):
        return b_part(((y + k) & (NY - 1)) * NZ + z, sent.at[3], b_recv.at[1, z], at_z(d))

    def row_copy(d):
        return copy(colg.at[p], colg.at[p], sent.at[4], group_recv.at[0], at_row(d))

    def meta_copy(d):
        return copy(meta.at[y], meta.at[y], sent.at[5], group_recv.at[1], at_y(d))

    def a_phase(slot):
        for d in range(2):
            gath_u[slot, d] = to_phase(gath[slot, d], periods[d])

    def b_phase(slot):
        gath_u[slot, 2] = to_phase(gath[slot, 2], periods[2])

    reads[0].wait()
    for b in range(OWN):
        for d in range(3):
            v = pos[d : d + 1, b * BLK : (b + 1) * BLK]
            gath[q, d, b : b + 1, :] = v
            colg[p, d, b : b + 1, :] = v
    lane = lax.broadcasted_iota(jnp.int32, (8, BLK), 1)
    sub = lax.broadcasted_iota(jnp.int32, (8, BLK), 0)
    index = (lane + sub) & (BLK - 1)

    pl.semaphore_wait(barrier, len(peers))
    for d in y_order:
        b_first(d).start()
    for d in z_order[:2]:
        a_first(d).start()
    for d in y_order:
        a_then(0, d).start()
    for d in z_order[2:]:
        a_first(d).start()
    for d in z_order:
        b_then(0, d).start()
    for d in range(1, NR):
        row_copy(d).start()
    for read in reads[1:]:
        read.wait()
    meta[y] = jnp.full((8, BLK), -1.0, jnp.float32)
    meta[y, 0:1, 0:FAR] = tlv[0:1, OWN : OWN + FAR].astype(jnp.float32)

    for d in y_order:
        meta_copy(d).start()

    for d in range(3):
        u = to_phase(gath[q, d], periods[d])
        gath_u[q, d] = u
        colg_u[p, d] = u

    def pass_a(i, carry):
        k = z_step(i)
        slot = slot_of(0, k)
        arrived(a_recv.at[0, (z + k) & (NZ - 1)], gath.at[slot, pl.ds(0, 2)])
        for d in y_order:
            a_then(k, d).start()
        a_phase(slot)
        return carry

    def pass_b(k):
        slot = slot_of(k, 0)
        arrived(b_recv.at[0, (y + k) & (NY - 1)], gath.at[slot, 2])
        for d in z_order:
            b_then(k, d).start()
        b_phase(slot)

    def z_step(i):
        half = (i >> 1) + 1
        return (half + (i & 1) * (NZ - 2 * half)) & (NZ - 1)

    lax.fori_loop(0, min(2, NZ - 1), pass_a, 0)
    for k in y_order[:2]:
        pass_b(k)
    lax.fori_loop(min(2, NZ - 1), min(4, NZ - 1), pass_a, 0)
    for k in y_order[2:]:
        pass_b(k)
    lax.fori_loop(min(4, NZ - 1), NZ - 1, pass_a, 0)

    arrived(group_recv.at[0], colg.at[pl.ds(0, NR - 1)])
    for i in range(1, NR):
        slot = (p + i) & (NR - 1)
        for d in range(3):
            colg_u[slot, d] = to_phase(colg[slot, d], periods[d])

    def a_rest(k):
        arrived(a_recv.at[1, (z + k) & (NZ - 1)], gath.at[pl.ds(0, NY - 1), pl.ds(0, 2)])
        for d in y_order:
            a_phase(slot_of(d, k))

    def rest(i, carry):
        k = z_step(i)
        arrived(b_recv.at[1, (z + k) & (NZ - 1)], gath.at[pl.ds(0, NY), 2])
        for d in range(NY):
            b_phase(slot_of(d, k))
        a_rest(k)
        return carry

    a_rest(0)
    lax.fori_loop(0, NZ - 1, rest, 0)

    def head(t, rowed, skewed):
        r = tl[0, OWN + t]
        c = tl[1, OWN + t]
        for d in range(3):
            row = jnp.broadcast_to(gath_u[r >> 4, d, pl.ds(r & 15, 1), :], (8, BLK))
            rowed[0, d] = row
            for k in range(1, 4):
                rowed[k, d] = pltpu.roll(row, BLK - 8 * k, 1)
            column = colg_u[c >> 4, d, pl.ds(c & 15, 1), :]
            for k, shift in enumerate(FAR_SHIFTS):
                skewed[k, d] = skew(column, shift)

    def r1_copy(b, d):
        return copy(
            prs.at[b, y], prs.at[b, y], sent.at[6], r1_recv.at[b // (BATCHES - 1)], at_y(d)
        )

    def far_step(t, rowed, skewed, next_rowed, next_skewed):
        before = jnp.maximum(t - 2, 0)
        for d in range(3):
            at = pl.ds(before % GROUP, 1)
            prs[before // GROUP, y, d, at, :] = fold(rolled[d])
            cparts[before // GROUP, d, at, :] = fold(unskew(rolled[3 + d], index))
        for d in range(3):
            rolled[d] = settle_row([held[k, d] for k in range(4)])
            rolled[3 + d] = settle_column([held[4 + k, d] for k in range(4)], FAR_SHIFTS)
        now = jnp.minimum(t, FAR - 1)
        r = tl[0, OWN + now]
        c = tl[1, OWN + now]
        same = p * (NY * NZ * OWN) + r == ((c >> 4) * (NY * NZ) + q) * OWN + (c & 15)
        extra = jnp.where((sub == 0) & same, 1e6, 0.0)
        rows = [[rowed[k, d] for d in range(3)] for k in range(4)]
        columns = [[skewed[k, d] for d in range(3)] for k in range(4)]
        to_rows, to_columns = meet(rows, columns, scales, extra, None)
        head(jnp.minimum(t + 1, FAR - 1), next_rowed, next_skewed)
        for k in range(4):
            for d in range(3):
                held[k, d] = to_rows[k][d]
                held[4 + k, d] = to_columns[k][d]

    def far_steps(i, carry):
        far_step(2 * i, rowed.at[0], skewed.at[0], rowed.at[1], skewed.at[1])
        far_step(2 * i + 1, rowed.at[1], skewed.at[1], rowed.at[0], skewed.at[0])
        return carry

    def batch(b, carry):
        start = b * (GROUP // 2)
        lax.fori_loop(start, start + jnp.where(b < BATCHES, GROUP // 2, 1), far_steps, 0)

        @pl.when(b > 0)
        def _():
            for d in y_order:
                r1_copy(b - 1, d).start()

        return carry

    held[...] = jnp.zeros_like(held)
    rolled[...] = jnp.zeros_like(rolled)
    head(0, rowed.at[0], skewed.at[0])
    lax.fori_loop(0, BATCHES + 1, batch, 0)

    r = tlv[0:1, OWN : OWN + FAR]
    c = tlv[1:2, OWN : OWN + FAR]
    same = p * (NY * NZ * OWN) + r == ((c >> 4) * (NY * NZ) + q) * OWN + (c & 15)
    rows = lax.broadcasted_iota(jnp.int32, (NR * OWN, FAR), 0)
    minus = jnp.where((rows == c) & jnp.logical_not(same), -1.0, 0.0).astype(jnp.bfloat16)
    for d in range(3):
        full = spread(minus, cparts[:, d].reshape(FAR, BLK))
        coltot[:, d] = full.reshape(NR, OWN, BLK)

    def rc_copy(d):
        to = (p + d) & (NR - 1)
        return copy(coltot.at[to], crs.at[p], sent.at[7], group_recv.at[2], at_row(d))

    for d in range(1, NR):
        rc_copy(d).start()

    arrived(sent.at[0], gath.at[pl.ds(0, NZ - 1), pl.ds(0, 2)])
    arrived(sent.at[1], gath.at[pl.ds(0, NZ * (NY - 1)), pl.ds(0, 2)])
    arrived(sent.at[2], gath.at[pl.ds(0, NY - 1), 2])
    arrived(sent.at[3], gath.at[pl.ds(0, NY * (NZ - 1)), 2])
    arrived(sent.at[4], colg.at[pl.ds(0, NR - 1)])
    arrived(sent.at[5], meta.at[pl.ds(0, NY - 1)])

    def self_tile(k):
        u = [gath_u[q, d, pl.ds(k, 1), :] for d in range(3)]
        wide = [jnp.broadcast_to(v, (8, BLK)) for v in u]
        rows = [wide, [pltpu.roll(v, BLK - 8, 1) for v in wide]]
        columns = [[skew(v, shift) for v in u] for shift in SELF_SHIFTS]
        to_rows, to_columns = meet(rows, columns, scales, None, sub < 7)
        for d in range(3):
            force = settle_row([v[d] for v in to_rows])
            force -= unskew(settle_column([v[d] for v in to_columns], SELF_SHIFTS), index)
            own_f[d, pl.ds(k, 1), :] = strength * fold(force)

    def self_tiles(i, carry):
        self_tile(2 * i)
        self_tile(2 * i + 1)
        return carry

    lax.fori_loop(0, OWN // 2, self_tiles, 0)

    arrived(group_recv.at[1], meta.at[pl.ds(0, NY - 1)])

    def chosen(lo, hi):
        names = jnp.concatenate(
            [meta[i, 0:1, b * GROUP : (b + 1) * GROUP] for b in range(lo, hi) for i in range(NY)],
            axis=1,
        )
        count = NY * GROUP * (hi - lo)
        mine = lax.broadcasted_iota(jnp.int32, (NZ * OWN, count), 0) + y * (NZ * OWN)
        return jnp.where(mine.astype(jnp.float32) == names, 1.0, 0.0).astype(jnp.bfloat16)

    last = BATCHES - 1
    early = chosen(0, last)
    late = chosen(last, BATCHES)
    arrived(r1_recv.at[0], prs.at[pl.ds(0, last), pl.ds(0, NY - 1)])
    for d in range(3):
        full = spread(early, prs[0:last, :, d].reshape(last * NY * GROUP, BLK))
        totals[:, d] = full.reshape(NZ, OWN, BLK)
    arrived(r1_recv.at[1], prs.at[last, pl.ds(0, NY - 1)])
    for d in range(3):
        full = spread(late, prs[last, :, d].reshape(NY * GROUP, BLK))
        totals[:, d] += full.reshape(NZ, OWN, BLK)

    def r2_copy(d):
        to = (z + d) & (NZ - 1)
        return copy(totals.at[to], rs2.at[z], sent.at[8], group_recv.at[3], at_z(d))

    for d in reversed(z_order):
        r2_copy(d).start()

    x = [gath[q, d] for d in range(3)]
    order = chain[...]
    order_t = jnp.transpose(order.astype(jnp.float32))
    lane_f = lax.broadcasted_iota(jnp.int32, (BLK, BLK), 1).astype(jnp.float32)
    sub_f = lax.broadcasted_iota(jnp.int32, (BLK, BLK), 0).astype(jnp.float32)
    for b in range(OWN):
        hit = order_t[:, b : b + 1] == lane_f
        inv[b : b + 1, :] = jnp.sum(jnp.where(hit, sub_f, 0.0), axis=0, keepdims=True)
    back = inv[...].astype(jnp.int32)
    ordered = [jnp.take_along_axis(v, order, axis=1, mode="promise_in_bounds") for v in x]
    bond = [pltpu.roll(v, BLK - 1, 1) - v for v in ordered]
    squared = bond[0] * bond[0] + bond[1] * bond[1] + bond[2] * bond[2]
    rank = lax.broadcasted_iota(jnp.int32, (OWN, BLK), 1) + 1
    stiffness = -spring / jnp.maximum(1.0 - squared / (bond_reach * bond_reach), 0.3)
    stiffness = jnp.where(rank % CHAIN != 0, stiffness, 0.0)
    for d in range(3):
        pulled = bond[d] * stiffness
        along = pltpu.roll(pulled, 1, 1) - pulled
        own_f[d] += jnp.take_along_axis(along, back, axis=1, mode="promise_in_bounds")

    arrived(sent.at[6], prs.at[:, pl.ds(0, NY - 1)])
    arrived(sent.at[7], crs.at[pl.ds(0, NR - 1)])
    arrived(group_recv.at[2], crs.at[pl.ds(0, NR - 1)])
    acc = [coltot[p, d] + totals[z, d] for d in range(3)]
    for i in range(1, NR):
        slot = (p + i) & (NR - 1)
        acc = [acc[d] + crs[slot, d] for d in range(3)]
    arrived(group_recv.at[3], rs2.at[pl.ds(0, NZ - 1)])
    for i in range(1, NZ):
        slot = (z + i) & (NZ - 1)
        acc = [acc[d] + rs2[slot, d] for d in range(3)]
    for d in range(3):
        total = strength * acc[d] + own_f[d]
        for b in range(OWN):
            out[d : d + 1, b * BLK : (b + 1) * BLK] = total[b : b + 1, :]
    arrived(sent.at[8], totals.at[pl.ds(0, NZ - 1)])


def on_device(NR, NY, NZ, positions, velocities, chain_order, tile_list):
    f32, i32 = jnp.float32, jnp.int32
    dma = pltpu.SemaphoreType.DMA
    in_hbm = pl.BlockSpec(memory_space=pltpu.HBM)
    forces = pl.pallas_call(
        functools.partial(kernel, NR, NY, NZ),
        out_shape=jax.ShapeDtypeStruct(positions.shape, f32),
        in_specs=[in_hbm] * 3,
        out_specs=pl.BlockSpec(memory_space=pltpu.VMEM),
        scratch_shapes=[
            pltpu.SMEM(tile_list.shape, i32),
            pltpu.VMEM(tile_list.shape, i32),
            pltpu.VMEM(positions.shape, f32),
            pltpu.VMEM((OWN, BLK), i32),
            pltpu.VMEM((NY * NZ, 3, OWN, BLK), f32),
            pltpu.VMEM((NR, 3, OWN, BLK), f32),
            pltpu.VMEM((NY * NZ, 3, OWN, BLK), i32),
            pltpu.VMEM((NR, 3, OWN, BLK), i32),
            pltpu.VMEM((2, 4, 3, 8, BLK), i32),
            pltpu.VMEM((2, 4, 3, 8, BLK), i32),
            pltpu.VMEM((8, 3, 8, BLK), f32),
            pltpu.VMEM((6, 8, BLK), f32),
            pltpu.VMEM((3, OWN, BLK), f32),
            pltpu.VMEM((OWN, BLK), f32),
            pltpu.VMEM((NY, 8, BLK), f32),
            pltpu.VMEM((BATCHES, NY, 3, GROUP, BLK), f32),
            pltpu.VMEM((BATCHES, 3, GROUP, BLK), f32),
            pltpu.VMEM((NZ, 3, OWN, BLK), f32),
            pltpu.VMEM((NR, 3, OWN, BLK), f32),
            pltpu.VMEM((NZ, 3, OWN, BLK), f32),
            pltpu.VMEM((NR, 3, OWN, BLK), f32),
            dma((4,)),
            dma((9,)),
            dma((2, NZ)),
            dma((2, max(NY, NZ))),
            dma((4,)),
            dma((2,)),
        ],
        compiler_params=pltpu.CompilerParams(
            collective_id=0, has_side_effects=True, vmem_limit_bytes=56 * 1024 * 1024
        ),
    )(tile_list, positions, chain_order)
    new_velocity = velocities + time_step * forces
    new_position = positions + time_step * new_velocity
    return (new_velocity, new_position)


def solution(mesh, NZ=8):
    in_specs = (
        P(None, ("row", "col")),
        P(None, ("row", "col")),
        P(("row", "col"), None),
        P(None, ("row", "col")),
    )
    out_specs = (P(None, ("row", "col")), P(None, ("row", "col")))
    return jax.shard_map(
        functools.partial(on_device, mesh.shape["row"], mesh.shape["col"] // NZ, NZ),
        mesh=mesh,
        in_specs=in_specs,
        out_specs=out_specs,
        check_vma=False,
    )
```

time: 565 us -> 40 us (0.07)
  waiting for transfers between devices: 333 us -> 0 us
  local copies, waits for them, and re-layouts: 75.3 us -> 0.01 us
  other arithmetic: 74 us -> 1.4 us
  blocking collectives: 66.7 us -> 0 us
  Pallas kernels: 0 us -> 37.2 us
  between operations: 14.2 us -> 0.67 us
    reduce_scatter x2 -> x0, waiting for transfers between devices: 333 us -> none  [the longest x1 321 us: on_device(): lax.psum_scatter(row_totals.reshape(3, -1), 'col', scatter_dimension=1, t...]
    all_gather x2 -> x0, blocking collectives: 66.7 us -> none  [the longest x1 53.6 us: on_device(): row_group = lax.all_gather(positions, 'col', axis=1, tiled=True)]
    reduce_sum x33 -> x0, other arithmetic: 37.9 us -> none  [the longest x16 21.1 us: pair_terms(): jnp.sum(pair_force, axis=1)]
    pallas_call x0 -> x1, Pallas kernels: none -> 37.2 us  [on_device(): pl.pallas_call(functools.partial(kernel, NR, NY, NZ), out_shape=jax.Shape...]
    gather x33 -> x0, local copies, waits for them, and re-layouts: 31.3 us -> none  [the longest x1 13 us: fene(): ordered = jnp.take_along_axis(block_positions, chain[None], axis=2)]
    scatter-add x32 -> x0, other arithmetic: 23.2 us -> none  [the longest x16 11.6 us: one_section(): row_totals.at[:, row_pick].add(row_part)]
    while x2 -> x0, local copies, waits for them, and re-layouts: 20.4 us -> none  [on_device(): lax.fori_loop(0, owned_blocks, one_section, (jnp.zeros_like(row_blocks),...]
    dynamic_slice x16 -> x0, local copies, waits for them, and re-layouts: 12.1 us -> none  [one_section(): lax.dynamic_slice_in_dim(tile_list, section * per_section, per_section, 1)]
  transfers between devices with their start and end apart: 2 -> 0, of which waited for: 2 -> 0; matrix products, arithmetic and copies ran while one was open for 7% -> 0% of each run, Pallas kernels for 0% -> 0%
where the time goes in v3:
time: 40 us; the launch traced here: 39.3 us
  Pallas kernels  37.2 us (93%)
  other arithmetic  1.4 us (4%)
  between operations  0.67 us (2%)
    pallas_call x1, Pallas kernels, on_device(): pl.pallas_call(functools.partial(kernel, NR, NY, NZ), out_shape=jax.Shape...  37.2 us
    add x1, other arithmetic, on_device(): new_position = positions + time_step * new_velocity  1.4 us

profile of v3, /device:TPU:6, one launch (start us, length us, event | category | flops | bytes accessed | tf_op | source)
XLA Modules:
  0.0 39.3 jit_solution(17162908241774603417)
XLA Ops:
  0.6 0.0 copy-start
  0.6 0.0 copy-start.1
  0.7 37.2 %shard_map.59 = f32[3,2048]{1,0:T(4,128)} custom-call(s32[2,80]{1,0:T(2,128)} %tl_any.1, f32[3,2048]{1,0:T(4,128)} %pos_any.1, s32[16,128]{1,0:T(8,128)} %chain_any.1), custom_call_target="tpu_custom_call" | custom-call | tf_op jit(solution)/shard_map/pallas_call | solution.py:460
  37.9 0.0 copy-done
  37.9 0.0 copy-done.1
  37.9 1.4 %multiply_add_fusion = (f32[3,2048]{1,0:T(4,128)}, f32[3,2048]{1,0:T(4,128)}) fusion(f32[3,2048]{1,0:T(4,128)S(1)} %copy-done, f32[3,2048]{1,0:T(4,128)S(1)} %copy-done.1, f32[3,2048]{1,0:T(4,128)} %shard_map.59), kind=kLoop, calls=%fused_computation | loop fusion | flops 24576 | bytes 122880 | tf_op jit(solution)/shard_map/add | solution.py:499
Async XLA Ops:
  0.6 37.3 %copy-start = (f32[3,2048]{1,0:T(4,128)S(1)}, f32[3,2048]{1,0:T(4,128)}, u32[]{:S(2)}) copy-start(f32[3,2048]{1,0:T(4,128)} %pos_any.1) | copy-start | bytes 73732
  0.6 37.3 %copy-start.1 = (f32[3,2048]{1,0:T(4,128)S(1)}, f32[3,2048]{1,0:T(4,128)}, u32[]{:S(2)}) copy-start(f32[3,2048]{1,0:T(4,128)} %param.5) | copy-start | bytes 73732

commit v4 on v3

--- a/solution.py
+++ b/solution.py
@@ -245,7 +245,7 @@
     def pass_b(k):
         slot = slot_of(k, 0)
         arrived(b_recv.at[0, (y + k) & (NY - 1)], gath.at[slot, 2])
-        for d in z_order:
+        for d in reversed(z_order):
             b_then(k, d).start()
         b_phase(slot)
 

time: 40 us -> 39.3 us (0.982); the launches traced: 39.3 us -> 39.1 us
  no operation moved by 1% of the time
where the time goes in v4:
time: 39.3 us; the launch traced here: 39.1 us
  Pallas kernels  37 us (94%)
  other arithmetic  1.4 us (4%)
  between operations  0.67 us (2%)
    pallas_call x1, Pallas kernels, on_device(): pl.pallas_call(functools.partial(kernel, NR, NY, NZ), out_shape=jax.Shape...  37 us
    add x1, other arithmetic, on_device(): new_position = positions + time_step * new_velocity  1.4 us

profile of v4, /device:TPU:6, one launch (start us, length us, event | category | flops | bytes accessed | tf_op | source)
XLA Modules:
  0.0 39.1 jit_solution(9918457999948488955)
XLA Ops:
  0.6 0.0 copy-start
  0.6 0.0 copy-start.1
  0.7 37.0 %shard_map.59 = f32[3,2048]{1,0:T(4,128)} custom-call(s32[2,80]{1,0:T(2,128)} %tl_any.1, f32[3,2048]{1,0:T(4,128)} %pos_any.1, s32[16,128]{1,0:T(8,128)} %chain_any.1), custom_call_target="tpu_custom_call" | custom-call | tf_op jit(solution)/shard_map/pallas_call | solution.py:460
  37.7 0.0 copy-done
  37.7 0.0 copy-done.1
  37.7 1.4 %multiply_add_fusion = (f32[3,2048]{1,0:T(4,128)}, f32[3,2048]{1,0:T(4,128)}) fusion(f32[3,2048]{1,0:T(4,128)S(1)} %copy-done, f32[3,2048]{1,0:T(4,128)S(1)} %copy-done.1, f32[3,2048]{1,0:T(4,128)} %shard_map.59), kind=kLoop, calls=%fused_computation | loop fusion | flops 24576 | bytes 122880 | tf_op jit(solution)/shard_map/add | solution.py:499
Async XLA Ops:
  0.6 37.1 %copy-start = (f32[3,2048]{1,0:T(4,128)S(1)}, f32[3,2048]{1,0:T(4,128)}, u32[]{:S(2)}) copy-start(f32[3,2048]{1,0:T(4,128)} %pos_any.1) | copy-start | bytes 73732
  0.6 37.1 %copy-start.1 = (f32[3,2048]{1,0:T(4,128)S(1)}, f32[3,2048]{1,0:T(4,128)}, u32[]{:S(2)}) copy-start(f32[3,2048]{1,0:T(4,128)} %param.5) | copy-start | bytes 73732

commit v5 on v4

--- a/solution.py
+++ b/solution.py
@@ -301,6 +301,7 @@
         )
 
     def far_step(t, rowed, skewed, next_rowed, next_skewed):
+        head(jnp.minimum(t + 1, FAR - 1), next_rowed, next_skewed)
         before = jnp.maximum(t - 2, 0)
         for d in range(3):
             at = pl.ds(before % GROUP, 1)
@@ -317,7 +318,6 @@
         rows = [[rowed[k, d] for d in range(3)] for k in range(4)]
         columns = [[skewed[k, d] for d in range(3)] for k in range(4)]
         to_rows, to_columns = meet(rows, columns, scales, extra, None)
-        head(jnp.minimum(t + 1, FAR - 1), next_rowed, next_skewed)
         for k in range(4):
             for d in range(3):
                 held[k, d] = to_rows[k][d]
@@ -492,9 +492,9 @@
             dma((2,)),
         ],
         compiler_params=pltpu.CompilerParams(
-            collective_id=0, has_side_effects=True, vmem_limit_bytes=56 * 1024 * 1024
+            collective_id=0, has_side_effects=True, vmem_limit_bytes=32 * 1024 * 1024
         ),
-    )(tile_list, positions, chain_order)
+    )(*[pltpu.with_memory_space_constraint(v, pltpu.HBM) for v in (tile_list, positions, chain_order)])
     new_velocity = velocities + time_step * forces
     new_position = positions + time_step * new_velocity
     return (new_velocity, new_position)

time: 39.3 us -> 37.8 us (0.962)
  other arithmetic: 1.4 us -> 0.65 us
  Pallas kernels: 37 us -> 36.3 us
    add x1, other arithmetic: 1.4 us -> 0.65 us  [on_device(): new_position = positions + time_step * new_velocity]
    pallas_call x1, Pallas kernels: 37 us -> 36.3 us  [on_device(): pl.pallas_call(functools.partial(kernel, NR, NY, NZ), out_shape=jax.Shape...]
where the time goes in v5:
time: 37.8 us; the launch traced here: 37.6 us
  Pallas kernels  36.3 us (96%)
  between operations  0.67 us (2%)
  other arithmetic  0.65 us (2%)
    pallas_call x1, Pallas kernels, on_device(): pl.pallas_call(functools.partial(kernel, NR, NY, NZ), out_shape=jax.Shape...  36.3 us

profile of v5, /device:TPU:6, one launch (start us, length us, event | category | flops | bytes accessed | tf_op | source)
XLA Modules:
  0.0 37.6 jit_solution(14842019190775758676)
XLA Ops:
  0.6 0.0 copy-start
  0.6 0.0 copy-start.1
  0.7 36.3 %shard_map.59 = f32[3,2048]{1,0:T(4,128)S(1)} custom-call(s32[2,80]{1,0:T(2,128)} %tl_any.1, f32[3,2048]{1,0:T(4,128)} %pos_any.1, s32[16,128]{1,0:T(8,128)} %chain_any.1), custom_call_target="tpu_custom_call" | custom-call | tf_op jit(solution)/shard_map/pallas_call | solution.py:460
  36.9 0.0 copy-done
  37.0 0.0 copy-done.1
  37.0 0.6 %multiply_add_fusion = (f32[3,2048]{1,0:T(4,128)}, f32[3,2048]{1,0:T(4,128)}) fusion(f32[3,2048]{1,0:T(4,128)S(1)} %copy-done, f32[3,2048]{1,0:T(4,128)S(1)} %copy-done.1, f32[3,2048]{1,0:T(4,128)S(1)} %shard_map.59), kind=kLoop, calls=%fused_computation | loop fusion | flops 24576 | bytes 122880 | tf_op jit(solution)/shard_map/add | solution.py:499
Async XLA Ops:
  0.6 36.3 %copy-start = (f32[3,2048]{1,0:T(4,128)S(1)}, f32[3,2048]{1,0:T(4,128)}, u32[]{:S(2)}) copy-start(f32[3,2048]{1,0:T(4,128)} %pos_any.1) | copy-start | bytes 73732
  0.6 36.3 %copy-start.1 = (f32[3,2048]{1,0:T(4,128)S(1)}, f32[3,2048]{1,0:T(4,128)}, u32[]{:S(2)}) copy-start(f32[3,2048]{1,0:T(4,128)} %param.5) | copy-start | bytes 73732

commit v6 on v5

--- a/solution.py
+++ b/solution.py
@@ -176,19 +176,19 @@
 
     def a_then(k, d):
         far_z = (z + k) & (NZ - 1)
-        return a_part(y * NZ + far_z, sent.at[1], a_recv.at[1, far_z], at_y(d))
+        return a_part(y * NZ + far_z, sent.at[0], a_recv.at[1, far_z], at_y(d))
 
     def b_first(d):
-        return b_part(q, sent.at[2], b_recv.at[0, y], at_y(d))
+        return b_part(q, sent.at[1], b_recv.at[y], at_y(d))
 
     def b_then(k, d):
-        return b_part(((y + k) & (NY - 1)) * NZ + z, sent.at[3], b_recv.at[1, z], at_z(d))
+        return b_part(((y + k) & (NY - 1)) * NZ + z, sent.at[1], a_recv.at[1, z], at_z(d))
 
     def row_copy(d):
-        return copy(colg.at[p], colg.at[p], sent.at[4], group_recv.at[0], at_row(d))
+        return copy(colg.at[p], colg.at[p], sent.at[2], group_recv.at[0], at_row(d))
 
     def meta_copy(d):
-        return copy(meta.at[y], meta.at[y], sent.at[5], group_recv.at[1], at_y(d))
+        return copy(meta.at[y], meta.at[y], sent.at[3], group_recv.at[1], at_y(d))
 
     def a_phase(slot):
         for d in range(2):
@@ -216,10 +216,10 @@
         a_then(0, d).start()
     for d in z_order[2:]:
         a_first(d).start()
+    for d in range(1, NR):
+        row_copy(d).start()
     for d in z_order:
         b_then(0, d).start()
-    for d in range(1, NR):
-        row_copy(d).start()
     for read in reads[1:]:
         read.wait()
     meta[y] = jnp.full((8, BLK), -1.0, jnp.float32)
@@ -244,7 +244,7 @@
 
     def pass_b(k):
         slot = slot_of(k, 0)
-        arrived(b_recv.at[0, (y + k) & (NY - 1)], gath.at[slot, 2])
+        arrived(b_recv.at[(y + k) & (NY - 1)], gath.at[slot, 2])
         for d in reversed(z_order):
             b_then(k, d).start()
         b_phase(slot)
@@ -268,18 +268,18 @@
             colg_u[slot, d] = to_phase(colg[slot, d], periods[d])
 
     def a_rest(k):
-        arrived(a_recv.at[1, (z + k) & (NZ - 1)], gath.at[pl.ds(0, NY - 1), pl.ds(0, 2)])
         for d in y_order:
             a_phase(slot_of(d, k))
 
     def rest(i, carry):
         k = z_step(i)
-        arrived(b_recv.at[1, (z + k) & (NZ - 1)], gath.at[pl.ds(0, NY), 2])
+        arrived(a_recv.at[1, (z + k) & (NZ - 1)], gath.at[pl.ds(0, 3 * NY - 2), 2])
         for d in range(NY):
             b_phase(slot_of(d, k))
         a_rest(k)
         return carry
 
+    arrived(a_recv.at[1, z], gath.at[pl.ds(0, NY - 1), pl.ds(0, 2)])
     a_rest(0)
     lax.fori_loop(0, NZ - 1, rest, 0)
 
@@ -297,22 +297,26 @@
 
     def r1_copy(b, d):
         return copy(
-            prs.at[b, y], prs.at[b, y], sent.at[6], r1_recv.at[b // (BATCHES - 1)], at_y(d)
+            prs.at[b, y], prs.at[b, y], sent.at[4], r1_recv.at[b // (BATCHES - 1)], at_y(d)
         )
 
-    def far_step(t, rowed, skewed, next_rowed, next_skewed):
-        head(jnp.minimum(t + 1, FAR - 1), next_rowed, next_skewed)
-        before = jnp.maximum(t - 2, 0)
+    def finish(t):
         for d in range(3):
-            at = pl.ds(before % GROUP, 1)
-            prs[before // GROUP, y, d, at, :] = fold(rolled[d])
-            cparts[before // GROUP, d, at, :] = fold(unskew(rolled[3 + d], index))
+            at = pl.ds(t % GROUP, 1)
+            prs[t // GROUP, y, d, at, :] = fold(rolled[d])
+            cparts[t // GROUP, d, at, :] = fold(unskew(rolled[3 + d], index))
+
+    def settle():
         for d in range(3):
             rolled[d] = settle_row([held[k, d] for k in range(4)])
             rolled[3 + d] = settle_column([held[4 + k, d] for k in range(4)], FAR_SHIFTS)
-        now = jnp.minimum(t, FAR - 1)
-        r = tl[0, OWN + now]
-        c = tl[1, OWN + now]
+
+    def far_step(t, rowed, skewed, next_rowed, next_skewed):
+        head(jnp.minimum(t + 1, FAR - 1), next_rowed, next_skewed)
+        finish(jnp.maximum(t - 2, 0))
+        settle()
+        r = tl[0, OWN + t]
+        c = tl[1, OWN + t]
         same = p * (NY * NZ * OWN) + r == ((c >> 4) * (NY * NZ) + q) * OWN + (c & 15)
         extra = jnp.where((sub == 0) & same, 1e6, 0.0)
         rows = [[rowed[k, d] for d in range(3)] for k in range(4)]
@@ -330,7 +334,7 @@
 
     def batch(b, carry):
         start = b * (GROUP // 2)
-        lax.fori_loop(start, start + jnp.where(b < BATCHES, GROUP // 2, 1), far_steps, 0)
+        lax.fori_loop(start, start + GROUP // 2, far_steps, 0)
 
         @pl.when(b > 0)
         def _():
@@ -342,7 +346,12 @@
     held[...] = jnp.zeros_like(held)
     rolled[...] = jnp.zeros_like(rolled)
     head(0, rowed.at[0], skewed.at[0])
-    lax.fori_loop(0, BATCHES + 1, batch, 0)
+    lax.fori_loop(0, BATCHES, batch, 0)
+    finish(FAR - 2)
+    settle()
+    finish(FAR - 1)
+    for d in reversed(y_order):
+        r1_copy(BATCHES - 1, d).start()
 
     r = tlv[0:1, OWN : OWN + FAR]
     c = tlv[1:2, OWN : OWN + FAR]
@@ -355,17 +364,15 @@
 
     def rc_copy(d):
         to = (p + d) & (NR - 1)
-        return copy(coltot.at[to], crs.at[p], sent.at[7], group_recv.at[2], at_row(d))
+        return copy(coltot.at[to], crs.at[p], sent.at[5], group_recv.at[2], at_row(d))
 
     for d in range(1, NR):
         rc_copy(d).start()
 
-    arrived(sent.at[0], gath.at[pl.ds(0, NZ - 1), pl.ds(0, 2)])
-    arrived(sent.at[1], gath.at[pl.ds(0, NZ * (NY - 1)), pl.ds(0, 2)])
-    arrived(sent.at[2], gath.at[pl.ds(0, NY - 1), 2])
-    arrived(sent.at[3], gath.at[pl.ds(0, NY * (NZ - 1)), 2])
-    arrived(sent.at[4], colg.at[pl.ds(0, NR - 1)])
-    arrived(sent.at[5], meta.at[pl.ds(0, NY - 1)])
+    arrived(sent.at[0], gath.at[pl.ds(0, NY * NZ - 1), pl.ds(0, 2)])
+    arrived(sent.at[1], gath.at[pl.ds(0, NY * NZ - 1), 2])
+    arrived(sent.at[2], colg.at[pl.ds(0, NR - 1)])
+    arrived(sent.at[3], meta.at[pl.ds(0, NY - 1)])
 
     def self_tile(k):
         u = [gath_u[q, d, pl.ds(k, 1), :] for d in range(3)]
@@ -410,7 +417,7 @@
 
     def r2_copy(d):
         to = (z + d) & (NZ - 1)
-        return copy(totals.at[to], rs2.at[z], sent.at[8], group_recv.at[3], at_z(d))
+        return copy(totals.at[to], rs2.at[z], sent.at[6], group_recv.at[3], at_z(d))
 
     for d in reversed(z_order):
         r2_copy(d).start()
@@ -435,8 +442,8 @@
         along = pltpu.roll(pulled, 1, 1) - pulled
         own_f[d] += jnp.take_along_axis(along, back, axis=1, mode="promise_in_bounds")
 
-    arrived(sent.at[6], prs.at[:, pl.ds(0, NY - 1)])
-    arrived(sent.at[7], crs.at[pl.ds(0, NR - 1)])
+    arrived(sent.at[4], prs.at[:, pl.ds(0, NY - 1)])
+    arrived(sent.at[5], crs.at[pl.ds(0, NR - 1)])
     arrived(group_recv.at[2], crs.at[pl.ds(0, NR - 1)])
     acc = [coltot[p, d] + totals[z, d] for d in range(3)]
     for i in range(1, NR):
@@ -450,7 +457,7 @@
         total = strength * acc[d] + own_f[d]
         for b in range(OWN):
             out[d : d + 1, b * BLK : (b + 1) * BLK] = total[b : b + 1, :]
-    arrived(sent.at[8], totals.at[pl.ds(0, NZ - 1)])
+    arrived(sent.at[6], totals.at[pl.ds(0, NZ - 1)])
 
 
 def on_device(NR, NY, NZ, positions, velocities, chain_order, tile_list):
@@ -485,9 +492,9 @@
             pltpu.VMEM((NZ, 3, OWN, BLK), f32),
             pltpu.VMEM((NR, 3, OWN, BLK), f32),
             dma((4,)),
-            dma((9,)),
+            dma((7,)),
             dma((2, NZ)),
-            dma((2, max(NY, NZ))),
+            dma((NY,)),
             dma((4,)),
             dma((2,)),
         ],

time: 37.8 us -> 37.6 us (level)
  no operation moved by 1% of the time
where the time goes in v6:
time: 37.6 us; the launch traced here: 37.5 us
  Pallas kernels  36.2 us (96%)
  between operations  0.67 us (2%)
  other arithmetic  0.65 us (2%)
    pallas_call x1, Pallas kernels, on_device(): pl.pallas_call(functools.partial(kernel, NR, NY, NZ), out_shape=jax.Shape...  36.2 us

profile of v6, /device:TPU:6, one launch (start us, length us, event | category | flops | bytes accessed | tf_op | source)
XLA Modules:
  0.0 37.5 jit_solution(10705177988070695157)
XLA Ops:
  0.6 0.0 copy-start
  0.6 0.0 copy-start.1
  0.7 36.2 %shard_map.59 = f32[3,2048]{1,0:T(4,128)S(1)} custom-call(s32[2,80]{1,0:T(2,128)} %tl_any.1, f32[3,2048]{1,0:T(4,128)} %pos_any.1, s32[16,128]{1,0:T(8,128)} %chain_any.1), custom_call_target="tpu_custom_call" | custom-call | tf_op jit(solution)/shard_map/pallas_call | solution.py:467
  36.8 0.0 copy-done
  36.8 0.0 copy-done.1
  36.8 0.6 %multiply_add_fusion = (f32[3,2048]{1,0:T(4,128)}, f32[3,2048]{1,0:T(4,128)}) fusion(f32[3,2048]{1,0:T(4,128)S(1)} %copy-done, f32[3,2048]{1,0:T(4,128)S(1)} %copy-done.1, f32[3,2048]{1,0:T(4,128)S(1)} %shard_map.59), kind=kLoop, calls=%fused_computation | loop fusion | flops 24576 | bytes 122880 | tf_op jit(solution)/shard_map/add | solution.py:506
Async XLA Ops:
  0.6 36.2 %copy-start = (f32[3,2048]{1,0:T(4,128)S(1)}, f32[3,2048]{1,0:T(4,128)}, u32[]{:S(2)}) copy-start(f32[3,2048]{1,0:T(4,128)} %pos_any.1) | copy-start | bytes 73732
  0.6 36.2 %copy-start.1 = (f32[3,2048]{1,0:T(4,128)S(1)}, f32[3,2048]{1,0:T(4,128)}, u32[]{:S(2)}) copy-start(f32[3,2048]{1,0:T(4,128)} %param.5) | copy-start | bytes 73732

commit v7 on v6

--- a/solution.py
+++ b/solution.py
@@ -208,14 +208,12 @@
     index = (lane + sub) & (BLK - 1)
 
     pl.semaphore_wait(barrier, len(peers))
+    for d in z_order:
+        a_first(d).start()
     for d in y_order:
         b_first(d).start()
-    for d in z_order[:2]:
-        a_first(d).start()
     for d in y_order:
         a_then(0, d).start()
-    for d in z_order[2:]:
-        a_first(d).start()
     for d in range(1, NR):
         row_copy(d).start()
     for d in z_order:
@@ -261,6 +259,8 @@
         pass_b(k)
     lax.fori_loop(min(4, NZ - 1), NZ - 1, pass_a, 0)
 
+    held[...] = jnp.zeros_like(held)
+    rolled[...] = jnp.zeros_like(rolled)
     arrived(group_recv.at[0], colg.at[pl.ds(0, NR - 1)])
     for i in range(1, NR):
         slot = (p + i) & (NR - 1)
@@ -343,8 +343,6 @@
 
         return carry
 
-    held[...] = jnp.zeros_like(held)
-    rolled[...] = jnp.zeros_like(rolled)
     head(0, rowed.at[0], skewed.at[0])
     lax.fori_loop(0, BATCHES, batch, 0)
     finish(FAR - 2)

time: 37.6 us -> 37.6 us (level)
  no operation moved by 1% of the time
where the time goes in v7:
time: 37.6 us; the launch traced here: 37.5 us
  Pallas kernels  36.1 us (96%)
  between operations  0.67 us (2%)
  other arithmetic  0.65 us (2%)
    pallas_call x1, Pallas kernels, on_device(): pl.pallas_call(functools.partial(kernel, NR, NY, NZ), out_shape=jax.Shape...  36.1 us

profile of v7, /device:TPU:6, one launch (start us, length us, event | category | flops | bytes accessed | tf_op | source)
XLA Modules:
  0.0 37.5 jit_solution(16987526546353872314)
XLA Ops:
  0.6 0.0 copy-start
  0.6 0.0 copy-start.1
  0.7 36.1 %shard_map.59 = f32[3,2048]{1,0:T(4,128)S(1)} custom-call(s32[2,80]{1,0:T(2,128)} %tl_any.1, f32[3,2048]{1,0:T(4,128)} %pos_any.1, s32[16,128]{1,0:T(8,128)} %chain_any.1), custom_call_target="tpu_custom_call" | custom-call | tf_op jit(solution)/shard_map/pallas_call | solution.py:465
  36.8 0.0 copy-done
  36.8 0.0 copy-done.1
  36.8 0.6 %multiply_add_fusion = (f32[3,2048]{1,0:T(4,128)}, f32[3,2048]{1,0:T(4,128)}) fusion(f32[3,2048]{1,0:T(4,128)S(1)} %copy-done, f32[3,2048]{1,0:T(4,128)S(1)} %copy-done.1, f32[3,2048]{1,0:T(4,128)S(1)} %shard_map.59), kind=kLoop, calls=%fused_computation | loop fusion | flops 24576 | bytes 122880 | tf_op jit(solution)/shard_map/add | solution.py:504
Async XLA Ops:
  0.6 36.2 %copy-start = (f32[3,2048]{1,0:T(4,128)S(1)}, f32[3,2048]{1,0:T(4,128)}, u32[]{:S(2)}) copy-start(f32[3,2048]{1,0:T(4,128)} %pos_any.1) | copy-start | bytes 73732
  0.6 36.2 %copy-start.1 = (f32[3,2048]{1,0:T(4,128)S(1)}, f32[3,2048]{1,0:T(4,128)}, u32[]{:S(2)}) copy-start(f32[3,2048]{1,0:T(4,128)} %param.5) | copy-start | bytes 73732

commit v8 on v7

--- a/solution.py
+++ b/solution.py
@@ -208,10 +208,10 @@
     index = (lane + sub) & (BLK - 1)
 
     pl.semaphore_wait(barrier, len(peers))
+    for d in y_order:
+        b_first(d).start()
     for d in z_order:
         a_first(d).start()
-    for d in y_order:
-        b_first(d).start()
     for d in y_order:
         a_then(0, d).start()
     for d in range(1, NR):

time: 37.6 us -> 37.6 us (level)
  no operation moved by 1% of the time
where the time goes in v8:
time: 37.6 us; the launch traced here: 37.5 us
  Pallas kernels  36.2 us (96%)
  between operations  0.67 us (2%)
  other arithmetic  0.65 us (2%)
    pallas_call x1, Pallas kernels, on_device(): pl.pallas_call(functools.partial(kernel, NR, NY, NZ), out_shape=jax.Shape...  36.2 us

profile of v8, /device:TPU:6, one launch (start us, length us, event | category | flops | bytes accessed | tf_op | source)
XLA Modules:
  0.0 37.5 jit_solution(10516915865026695355)
XLA Ops:
  0.6 0.0 copy-start
  0.6 0.0 copy-start.1
  0.7 36.2 %shard_map.59 = f32[3,2048]{1,0:T(4,128)S(1)} custom-call(s32[2,80]{1,0:T(2,128)} %tl_any.1, f32[3,2048]{1,0:T(4,128)} %pos_any.1, s32[16,128]{1,0:T(8,128)} %chain_any.1), custom_call_target="tpu_custom_call" | custom-call | tf_op jit(solution)/shard_map/pallas_call | solution.py:465
  36.8 0.0 copy-done
  36.8 0.0 copy-done.1
  36.8 0.6 %multiply_add_fusion = (f32[3,2048]{1,0:T(4,128)}, f32[3,2048]{1,0:T(4,128)}) fusion(f32[3,2048]{1,0:T(4,128)S(1)} %copy-done, f32[3,2048]{1,0:T(4,128)S(1)} %copy-done.1, f32[3,2048]{1,0:T(4,128)S(1)} %shard_map.59), kind=kLoop, calls=%fused_computation | loop fusion | flops 24576 | bytes 122880 | tf_op jit(solution)/shard_map/add | solution.py:504
Async XLA Ops:
  0.6 36.2 %copy-start = (f32[3,2048]{1,0:T(4,128)S(1)}, f32[3,2048]{1,0:T(4,128)}, u32[]{:S(2)}) copy-start(f32[3,2048]{1,0:T(4,128)} %pos_any.1) | copy-start | bytes 73732
  0.6 36.2 %copy-start.1 = (f32[3,2048]{1,0:T(4,128)S(1)}, f32[3,2048]{1,0:T(4,128)}, u32[]{:S(2)}) copy-start(f32[3,2048]{1,0:T(4,128)} %param.5) | copy-start | bytes 73732
